TPU v7x, 32 devices: a whole 2x2x4 slice. The times are simulated.
32 devices in a mesh: rows: 4 (over y, x), cols: 8 (over z, core).
Axes of the slice: x: 2, y: 2, z: 4, core: 2. Of those that a mesh axis runs over, the one named last changes fastest.
Arguments:
- features: bfloat16 [2, 4096, 100], P(None, ('rows', 'cols')), may hold values from -6 to 6
- adjacency: bfloat16 [2, 4096, 4, 8, 128], P(None, 'rows', None, 'cols'), may hold values from -0.125 to 0.125
- block_mask: int32 [2, 32, 4, 8, 1], P(None, 'rows', None, 'cols'), may hold values 0 or 1
- diagonal: float32 [2, 4096], P(None, ('rows', 'cols')), may hold values from 0.2 to 1
- labels: int32 [2, 4096], P(None, ('rows', 'cols')), may hold values from 0 to 46
- train_mask: int32 [2, 4096], P(None, ('rows', 'cols')), may hold values from 0 to 1, as said below
- params: float32 [4501504], P(('rows', 'cols')), as said below
- first_moment: float32 [4501504], P(('rows', 'cols'))
- second_moment: float32 [4501504], P(('rows', 'cols')), as said below
Outputs:
- new_params: float32 [4501504], P(('rows', 'cols'))
- new_first: float32 [4501504], P(('rows', 'cols'))
- new_second: float32 [4501504], P(('rows', 'cols'))
- grad_norm: float32 [], replicated
- loss_sum: float32 [], replicated
- node_total: float32 [], replicated
- class_bias_grad: float32 [47], replicated
Inputs may be any that keep to these rules, and one draw needn't show every extreme that they name: `train_mask`: the share of ones rises with the node's index within a micro-batch. `params`: entries beyond 4499503 are padding. `second_moment`: positive.
All inputs are finite; a program needn't handle non-finite values. No bound on the sum of `block_mask` on one device may be relied on, other than what follows from the above.
Results may differ from a plain program's by a relative error of at most 0.0068.
Values may be sent and summed in bfloat16 or wider, within the bound.
No kernel may reach another device: no remote copies, remote signals or barrier semaphores. Data moves between devices by JAX's collectives and lax.ppermute only.
A program may use at most 192 MiB of HBM per device.

v0:
```python
import jax
import jax.numpy as jnp
from jax import lax
from jax.sharding import PartitionSpec as P

FIN = 100
HID = 2048
NCLS = 47
BLK = 128
MB = 2
STEP = 10


LAMBDA = 1.0
CLIP_NORM = 0.01
BETA_ONE = 0.9
BETA_TWO = 0.95
EPSILON = 1e-08
WEIGHT_DECAY = 0.1
LEARN_RATE = 0.02


def split_weights(flat_params):
    offset_two = FIN * HID
    offset_three = offset_two + HID * HID
    offset_bias = offset_three + HID * NCLS
    w_first = flat_params[:offset_two].reshape(FIN, HID)
    w_second = flat_params[offset_two:offset_three].reshape(HID, HID)
    w_third = flat_params[offset_three:offset_bias].reshape(HID, NCLS)
    b_first = flat_params[offset_bias : offset_bias + HID]
    b_second = flat_params[offset_bias + HID : offset_bias + 2 * HID]
    b_third = flat_params[offset_bias + 2 * HID : offset_bias + 2 * HID + NCLS]
    return (w_first, w_second, w_third, b_first, b_second, b_third)


def gather_weights(params):
    gathered = lax.all_gather(params.astype(jnp.bfloat16), ("rows", "cols"), axis=0, tiled=True)
    return split_weights(gathered)


def reduce_grads(local_grads):
    return lax.psum_scatter(local_grads, ("rows", "cols"), scatter_dimension=0, tiled=True)


def expand_blocks(blocks, block_side):
    block_rows, row_parts, single, block_cols = blocks.shape
    grown = jnp.broadcast_to(
        blocks[:, None, :, :, :, None],
        (block_rows, block_side, row_parts, single, block_cols, block_side),
    )
    return grown.reshape(block_rows * block_side, row_parts * single * block_cols * block_side)


def contract_rows(left, right):
    return lax.dot_general(
        left, right, (((0,), (0,)), ((), ())), preferred_element_type=jnp.float32
    )


def aggregate(fwd_tile, diag_vals, inputs):
    gathered = lax.all_gather(inputs, "rows", axis=0, tiled=True)
    summed = lax.psum_scatter(
        jnp.dot(fwd_tile, gathered, preferred_element_type=jnp.float32),
        "cols",
        scatter_dimension=0,
        tiled=True,
    )
    return summed + LAMBDA * diag_vals[:, None] * inputs.astype(jnp.float32)


def aggregate_back(adj_tile, diag_vals, upstream):
    row_grads = lax.all_gather(upstream, "cols", axis=0, tiled=True)
    summed = lax.psum_scatter(
        contract_rows(adj_tile, row_grads).astype(jnp.bfloat16),
        "rows",
        scatter_dimension=0,
        tiled=True,
    ).astype(jnp.float32)
    return summed + LAMBDA * diag_vals[:, None] * upstream.astype(jnp.float32)


def layer_forward(fwd_tile, diag_vals, hidden, weight, bias_row, agg_order):
    inputs = hidden.astype(jnp.bfloat16)
    if agg_order == "first":
        summed = aggregate(fwd_tile, diag_vals, inputs).astype(jnp.bfloat16)
        return (
            jnp.dot(summed, weight, preferred_element_type=jnp.float32)
            + bias_row.astype(jnp.float32),
            summed,
        )
    projected = jnp.dot(inputs, weight, preferred_element_type=jnp.float32).astype(jnp.bfloat16)
    return (aggregate(fwd_tile, diag_vals, projected) + bias_row.astype(jnp.float32), inputs)


def layer_backward(adj_tile, diag_vals, saved_input, weight, grad_out, agg_order, want_input):
    bias_grad = jnp.sum(grad_out, axis=0)
    grad_low = grad_out.astype(jnp.bfloat16)
    if agg_order == "first":
        weight_grad = contract_rows(saved_input, grad_low)
        if not want_input:
            return (weight_grad, bias_grad, None)
        inner = lax.dot_general(
            grad_low, weight, (((1,), (1,)), ((), ())), preferred_element_type=jnp.float32
        ).astype(jnp.bfloat16)
        return (weight_grad, bias_grad, aggregate_back(adj_tile, diag_vals, inner))
    proj_grad = aggregate_back(adj_tile, diag_vals, grad_low).astype(jnp.bfloat16)
    weight_grad = contract_rows(saved_input, proj_grad)
    input_grad = lax.dot_general(
        proj_grad, weight, (((1,), (1,)), ((), ())), preferred_element_type=jnp.float32
    )
    return (weight_grad, bias_grad, input_grad)


def gelu_back(pre_act, upstream):
    return jax.vjp(jax.nn.gelu, pre_act)[1](upstream)[0]


def per_device(
    features,
    adjacency,
    block_mask,
    diagonal,
    labels,
    train_mask,
    params,
    first_moment,
    second_moment,
):
    node_total = lax.psum(jnp.sum(train_mask.astype(jnp.float32)), ("rows", "cols"))
    full_length = params.shape[0] * lax.axis_size(("rows", "cols"))
    padding = full_length - (FIN * HID + HID * HID + HID * NCLS + 2 * HID + NCLS)
    loss_total = jnp.float32(0.0)
    class_total = jnp.zeros((NCLS,), jnp.float32)
    accumulated = jnp.zeros((full_length,), jnp.float32)
    for batch_index in range(MB):
        weights = gather_weights(params)
        w_first, w_second, w_third, b_first, b_second, b_third = weights
        adj_tile = adjacency[batch_index].reshape(adjacency.shape[1], -1) * expand_blocks(
            block_mask[batch_index], BLK
        ).astype(jnp.bfloat16)
        diag_vals = diagonal[batch_index]
        pre_one, saved_one = layer_forward(
            adj_tile, diag_vals, features[batch_index], w_first, b_first, "first"
        )
        hidden = jax.nn.gelu(pre_one)
        pre_two, saved_two = layer_forward(adj_tile, diag_vals, hidden, w_second, b_second, "first")
        hidden = jax.nn.gelu(pre_two)
        logits, saved_three = layer_forward(adj_tile, diag_vals, hidden, w_third, b_third, "last")
        log_total = jax.nn.logsumexp(logits, axis=1)
        label_hits = labels[batch_index][:, None] == jnp.arange(NCLS, dtype=jnp.int32)[None, :]
        picked = jnp.sum(jnp.where(label_hits, logits, 0.0), axis=1)
        counted = train_mask[batch_index].astype(jnp.float32)
        loss_total = loss_total + jnp.sum(counted * (log_total - picked))
        grad_logits = (
            counted[:, None]
            * (jnp.exp(logits - log_total[:, None]) - label_hits.astype(jnp.float32))
            / node_total
        )
        grad_w3, grad_b3, upstream = layer_backward(
            adj_tile, diag_vals, saved_three, w_third, grad_logits, "last", True
        )
        grad_w2, grad_b2, upstream = layer_backward(
            adj_tile, diag_vals, saved_two, w_second, gelu_back(pre_two, upstream), "first", True
        )
        grad_w1, grad_b1, unused = layer_backward(
            adj_tile, diag_vals, saved_one, w_first, gelu_back(pre_one, upstream), "first", False
        )
        class_total = class_total + grad_b3
        local_grads = jnp.concatenate(
            [
                grad_w1.reshape(-1),
                grad_w2.reshape(-1),
                grad_w3.reshape(-1),
                grad_b1,
                grad_b2,
                grad_b3,
                jnp.zeros((padding,), jnp.float32),
            ]
        )
        accumulated = accumulated + local_grads
    reduced = reduce_grads(accumulated)
    loss_sum, squares, class_sum = lax.psum(
        (loss_total, jnp.sum(reduced * reduced), class_total), ("rows", "cols")
    )
    grad_norm = jnp.sqrt(squares)
    clip_scale = jnp.minimum(1.0, CLIP_NORM / (grad_norm + 1e-06))
    clipped = reduced * clip_scale
    class_bias_grad = class_sum * clip_scale
    new_first = BETA_ONE * first_moment + (1.0 - BETA_ONE) * clipped
    new_second = BETA_TWO * second_moment + (1.0 - BETA_TWO) * clipped * clipped
    correct_one = 1.0 - BETA_ONE**STEP
    correct_two = 1.0 - BETA_TWO**STEP
    step_size = new_first / correct_one / (jnp.sqrt(new_second / correct_two) + EPSILON)
    new_params = params - LEARN_RATE * (step_size + WEIGHT_DECAY * params)
    return (new_params, new_first, new_second, grad_norm, loss_sum, node_total, class_bias_grad)


def solution(mesh):
    in_specs = (
        P(None, ("rows", "cols"), None),
        P(None, "rows", None, "cols", None),
        P(None, "rows", None, "cols", None),
        P(None, ("rows", "cols")),
        P(None, ("rows", "cols")),
        P(None, ("rows", "cols")),
        P(("rows", "cols")),
        P(("rows", "cols")),
        P(("rows", "cols")),
    )
    out_specs = (P(("rows", "cols")), P(("rows", "cols")), P(("rows", "cols")), P(), P(), P(), P())
    return jax.shard_map(
        per_device, mesh=mesh, in_specs=in_specs, out_specs=out_specs, check_vma=False
    )
```

profile of v0, /device:TPU:0, one launch (start us, length us, event | category | flops | bytes accessed | tf_op | source)
XLA Modules:
  0.0 1572.0 jit_solution(6143170941012148841)
XLA Ops:
  9.8 9.8 all-gather
  19.7 2.3 fusion.54
  22.5 1.2 fusion.35
  23.8 1.1 convert_element_type.181
  24.9 3.9 reshape.120
  29.0 8.3 all-gather.1
  38.0 1.2 fusion.33
  39.7 18.2 %reduce-scatter.15.cloned.1.call-done = f32[128,100]{0,1:T(8,128)} async-done(((f32[1024,100]{0,1:T(8,128)}), f32[128,100]{0,1:T(8,128)}) %reduce-scatter.15.cloned.1.call-update) | async-done | bytes 51216 | tf_op jit(solution)/shard_map/reduce_scatter | solution.py:62
  58.7 92.6 %all-gather.17.cloned.1.call-done = bf16[32,1,140672]{2,1,0:T(2,128)(2,1)} async-done(((bf16[1,1,140672]{2,1,0:T(2,128)(2,1)}), bf16[32,1,140672]{2,1,0:T(2,128)(2,1)}) %all-gather.17.cloned.1.call-update) | async-done | bytes 9003024 | tf_op jit(solution)/shard_map/all_gather | solution.py:37
  151.3 190.5 %reduce = bf16[32,140672]{1,0:T(8,128)(2,1)} reduce(bf16[32,1,140672]{2,1,0:T(2,128)(2,1)} %all-gather.17.cloned.1.call-done, bf16[]{:T(256)} %constant.50), dimensions={1}, to_apply=%all-gather.2.reduce_sub_computation | reduce | bytes 18006018 | tf_op jit(solution)/shard_map/all_gather | solution.py:37
  341.8 16.5 %reshape.121 = bf16[4501504]{0:T(1024)(128)(2,1)} reshape(bf16[32,140672]{1,0:T(8,128)(2,1)} %reduce) | data formatting | bytes 18006016
  358.4 1.0 slice.103
  360.3 1.7 multiply_convert_fusion.3
  362.9 1.7 multiply_convert_fusion.1
  364.8 30.8 %all-gather.9.cloned.1.call-done = bf16[512,2048]{1,0:T(8,128)(2,1)} async-done(((bf16[128,2048]{1,0:T(8,128)(2,1)}), bf16[512,2048]{1,0:T(8,128)(2,1)}) %all-gather.9.cloned.1.call-update) | async-done | bytes 2097168 | tf_op jit(solution)/shard_map/all_gather | solution.py:61
  395.7 7.2 fusion.59
  403.0 30.3 %all-gather.13.cloned.1.call-done = bf16[512,2048]{1,0:T(8,128)(2,1)} async-done(((bf16[128,2048]{1,0:T(8,128)(2,1)}), bf16[512,2048]{1,0:T(8,128)(2,1)}) %all-gather.13.cloned.1.call-update) | async-done | bytes 2097168 | tf_op jit(solution)/shard_map/all_gather | solution.py:61
  433.3 7.2 fusion.61
  441.1 41.3 %psum.28 = f32[]{:T(128)} all-reduce(f32[]{:T(128)} %convert_reduce_fusion), channel_id=1, replica_groups=mesh['rows'=4,'cols'=8] {'rows','cols'}, use_global_device_ids=true, to_apply=%region_6.0 | all-reduce | flops 1 | bytes 8 | tf_op jit(solution)/shard_map/psum | solution.py:129
  482.4 7.2 slice.105
  489.6 2.1 reshape.109
  491.8 13.4 slice.91
  505.1 21.0 %reduce-scatter.17.cloned.1.call-done = f32[128,2048]{1,0:T(8,128)} async-done(((f32[1024,2048]{1,0:T(8,128)}), f32[128,2048]{1,0:T(8,128)}) %reduce-scatter.17.cloned.1.call-update) | async-done | bytes 1048592 | tf_op jit(solution)/shard_map/reduce_scatter | solution.py:62
  526.1 90.2 %reduce-scatter.25.cloned.1.call-done = f32[128,2048]{1,0:T(8,128)} async-done(((f32[1024,2048]{1,0:T(8,128)}), f32[128,2048]{1,0:T(8,128)}) %reduce-scatter.25.cloned.1.call-update) | async-done | bytes 1048592 | tf_op jit(solution)/shard_map/reduce_scatter | solution.py:62
  616.3 2.1 add_convert_fusion
  618.4 4.7 convolution_add_fusion.2
  624.6 8.1 all_gather.42
  632.8 1.1 fusion.62
  634.0 4.7 convolution_add_fusion.3
  640.2 8.1 all_gather.37
  648.3 1.1 fusion.60
  650.2 11.6 reduce-scatter.27.cloned.1.call-done
  661.8 31.4 %reduce-scatter.19.cloned.1.call-done = f32[128,47]{0,1:T(8,128)} async-done(((f32[1024,47]{0,1:T(8,128)}), f32[128,47]{0,1:T(8,128)}) %reduce-scatter.19.cloned.1.call-update) | async-done | bytes 24080 | tf_op jit(solution)/shard_map/reduce_scatter | solution.py:62
  694.9 12.8 all_gather.38
  709.6 12.8 all_gather.43
  723.7 7.6 reduce-scatter.31.cloned.1.call-done
  732.1 2.3 fusion.57
  735.2 7.1 convolution_convert_fusion.3
  742.3 15.5 reduce-scatter.33.cloned.1.call-done
  758.7 2.3 fusion.58
  761.8 7.1 convolution_convert_fusion.2
  769.0 38.2 %all-gather.11.cloned.1.call-done = bf16[1024,2048]{1,0:T(8,128)(2,1)} async-done(((bf16[128,2048]{1,0:T(8,128)(2,1)}), bf16[1024,2048]{1,0:T(8,128)(2,1)}) %all-gather.11.cloned.1.call-update) | async-done | bytes 4194320 | tf_op jit(solution)/shard_map/all_gather | solution.py:72
  807.2 6.0 convolution_convert_fusion.1
  813.2 41.9 %all-gather.15.cloned.1.call-done = bf16[1024,2048]{1,0:T(8,128)(2,1)} async-done(((bf16[128,2048]{1,0:T(8,128)(2,1)}), bf16[1024,2048]{1,0:T(8,128)(2,1)}) %all-gather.15.cloned.1.call-update) | async-done | bytes 4194320 | tf_op jit(solution)/shard_map/all_gather | solution.py:72
  855.2 6.0 convolution_convert_fusion
  861.4 1.8 fusion.42
  863.2 1.4 reshape.115
  864.7 1.8 fusion.41
  866.5 1.4 reshape.112
  867.9 2.4 convolution_bitcast_fusion
  870.3 7.5 copy.47
  877.8 2.4 convolution_bitcast_fusion.1
  880.2 7.5 copy.44
  887.7 4.3 reduce-scatter.21.cloned.1.call-done
  892.1 2.0 fusion.51
  894.4 36.0 %reduce-scatter.29.cloned.1.call-done = bf16[128,2048]{1,0:T(8,128)(2,1)} async-done(((bf16[512,2048]{1,0:T(8,128)(2,1)}), bf16[128,2048]{1,0:T(8,128)(2,1)}) %reduce-scatter.29.cloned.1.call-update) | async-done | bytes 524304 | tf_op jit(solution)/shard_map/reduce_scatter | solution.py:73
  930.4 2.3 fusion.48
  933.1 135.8 %concatenate.7 = f32[4501504]{0:T(1024)} concatenate(f32[204800]{0:T(1024)S(1)} %reshape.113, f32[4194304]{0:T(1024)} %bitcast.101, f32[96256]{0:T(1024)S(1)} %copy-done.8, f32[2048]{0:T(1024)S(1)} %get-tuple-element.19, f32[2048]{0:T(1024)S(1)} %get-tuple-element.51, f32[47]{0:T(128)S(1)} %get-tuple-element.8, f32[2001]{0:T(1024)S(1)} %broadcast.58), dimensions={0} | concatenate | bytes 36012032 | tf_op jit(solution)/shard_map/concatenate | solution.py:169
  1068.9 136.4 %concatenate.6 = f32[4501504]{0:T(1024)} concatenate(f32[204800]{0:T(1024)S(1)} %reshape.110, f32[4194304]{0:T(1024)} %bitcast.100, f32[96256]{0:T(1024)S(1)} %copy-done.7, f32[2048]{0:T(1024)S(1)} %get-tuple-element.23, f32[2048]{0:T(1024)S(1)} %get-tuple-element.49, f32[47]{0:T(128)S(1)} %get-tuple-element.10, f32[2001]{0:T(1024)S(1)} %broadcast.58), dimensions={0} | concatenate | bytes 36012032 | tf_op jit(solution)/shard_map/concatenate | solution.py:169
  1205.3 18.7 %add.208 = f32[4501504]{0:T(1024)} add(f32[4501504]{0:T(1024)} %concatenate.6, f32[4501504]{0:T(1024)} %concatenate.7) | non-fusion elementwise | flops 4501504 | bytes 54018048 | tf_op jit(solution)/shard_map/add | solution.py:180
  1225.9 291.3 %all-reduce.4.cloned.1.call-done = f32[4501504]{0:T(1024)} async-done(((f32[4501504]{0:T(1024)}), f32[4501504]{0:T(1024)}) %all-reduce.4.cloned.1.call-update) | async-done | bytes 18006032
  1517.2 1.9 multiply_reduce_fusion
  1519.1 40.2 %all-reduce.1 = (f32[]{:T(128)}, f32[]{:T(128)}, f32[47]{0:T(128)S(1)}) all-reduce(f32[]{:T(128)} %multiply_reduce_fusion, f32[]{:T(128)S(6)} %add.215, f32[47]{0:T(128)S(1)} %add.216), channel_id=1, replica_groups=mesh['rows'=4,'cols'=8] {'rows','cols'}, use_global_device_ids=true, to_apply=%region_24.25 | all-reduce | flops 49 | bytes 392 | tf_op jit(solution)/shard_map/psum | solution.py:182
  1560.6 2.8 multiply_subtract_fusion
  (117 shorter events, 21.7 us)
Async XLA Ops:
  8.0 49.9 %reduce-scatter.15.cloned.1.call-start = ((), (), s32[]{:S(2)}) async-start(), calls=%async_computation.10 | async-start | bytes 479232 | tf_op jit(solution)/shard_map/reduce_scatter | solution.py:62
  21.9 17.8 %copy-start.17 = (f32[2,128]{1,0:T(2,128)S(1)}, f32[2,128]{1,0:T(2,128)}, u32[]{:S(2)}) copy-start(f32[2,128]{1,0:T(2,128)} %param.12) | copy-start | bytes 3076
  23.8 127.6 %all-gather.17.cloned.1.call-start = ((), (), s32[]{:S(2)}) async-start(), calls=%async_computation.22 | async-start | bytes 18568704 | tf_op jit(solution)/shard_map/all_gather | solution.py:37
  28.9 333.2 %reduce-scatter.23.cloned.1.call-start = ((), (), s32[]{:S(2)}) async-start(), calls=%async_computation.16 | async-start | bytes 479232 | tf_op jit(solution)/shard_map/reduce_scatter | solution.py:62
  39.2 356.5 %all-gather.9.cloned.1.call-start = ((), (), s32[]{:S(2)}) async-start(), calls=%async_computation.11 | async-start | bytes 2621440 | tf_op jit(solution)/shard_map/all_gather | solution.py:61
  362.0 71.3 %all-gather.13.cloned.1.call-start = ((), (), s32[]{:S(2)}) async-start(), calls=%async_computation.17 | async-start | bytes 2621440 | tf_op jit(solution)/shard_map/all_gather | solution.py:61
  364.6 161.5 %reduce-scatter.17.cloned.1.call-start = ((), (), s32[]{:S(2)}) async-start(), calls=%async_computation.12 | async-start | bytes 9437184 | tf_op jit(solution)/shard_map/reduce_scatter | solution.py:62
  402.9 37.6 %copy-start.16 = (s32[2,128]{1,0:T(2,128)S(1)}, s32[2,128]{1,0:T(2,128)}, u32[]{:S(2)}) copy-start(s32[2,128]{1,0:T(2,128)} %param.14) | copy-start | bytes 3076
  402.9 213.3 %reduce-scatter.25.cloned.1.call-start = ((), (), s32[]{:S(2)}) async-start(), calls=%async_computation.18 | async-start | bytes 9437184 | tf_op jit(solution)/shard_map/reduce_scatter | solution.py:62
  440.5 221.3 %reduce-scatter.27.cloned.1.call-start = ((), (), s32[]{:S(2)}) async-start(), calls=%async_computation.19 | async-start | bytes 221184 | tf_op jit(solution)/shard_map/reduce_scatter | solution.py:62
  482.4 7.2 slice-start
  618.4 5.7 copy-start.14
  623.2 1.0 copy-start.9
  633.9 59.3 %reduce-scatter.19.cloned.1.call-start = ((), (), s32[]{:S(2)}) async-start(), calls=%async_computation.13 | async-start | bytes 221184 | tf_op jit(solution)/shard_map/reduce_scatter | solution.py:62
  633.9 5.7 copy-start.15
  634.0 15.5 copy-start.18
  638.7 1.0 copy-start.10
  649.4 81.8 %reduce-scatter.31.cloned.1.call-start = ((), (), s32[]{:S(2)}) async-start(), calls=%async_computation.23 | async-start | bytes 163840
  708.7 49.1 %reduce-scatter.33.cloned.1.call-start = ((), (), s32[]{:S(2)}) async-start(), calls=%async_computation.24 | async-start | bytes 163840
  723.4 83.8 %all-gather.11.cloned.1.call-start = ((), (), s32[]{:S(2)}) async-start(), calls=%async_computation.14 | async-start | bytes 4718592 | tf_op jit(solution)/shard_map/all_gather | solution.py:72
  734.4 0.8 copy-start.3
  742.3 112.9 %all-gather.15.cloned.1.call-start = ((), (), s32[]{:S(2)}) async-start(), calls=%async_computation.20 | async-start | bytes 4718592 | tf_op jit(solution)/shard_map/all_gather | solution.py:72
  761.0 0.8 copy-start.5
  768.9 123.1 %reduce-scatter.21.cloned.1.call-start = ((), (), s32[]{:S(2)}) async-start(), calls=%async_computation.15 | async-start | bytes 2621440 | tf_op jit(solution)/shard_map/reduce_scatter | solution.py:73
  813.2 117.2 %reduce-scatter.29.cloned.1.call-start = ((), (), s32[]{:S(2)}) async-start(), calls=%async_computation.21 | async-start | bytes 2621440 | tf_op jit(solution)/shard_map/reduce_scatter | solution.py:73
  861.1 6.8 copy-start.6
  861.1 656.1 %all-reduce.4.cloned.1.call-start = ((), (), s32[]{:S(2)}) async-start(), calls=%async_computation.25 | async-start | bytes 36012032
  870.3 7.5 copy-start.4
  880.2 11.9 copy-start
  880.2 11.9 copy-start.11
  880.2 50.2 %copy-start.1 = (bf16[128,2048]{1,0:T(8,128)(2,1)S(1)}, bf16[128,2048]{1,0:T(8,128)(2,1)}, u32[]{:S(2)}) copy-start(bf16[128,2048]{1,0:T(8,128)(2,1)} %convolution_convert_fusion.2) | copy-start | bytes 1572868
  887.7 45.3 %copy-start.8 = (f32[96256]{0:T(1024)S(1)}, f32[96256]{0:T(1024)}, u32[]{:S(2)}) copy-start(f32[96256]{0:T(1024)} %reshape.115) | copy-start | bytes 1155076
  933.1 135.8 %copy-start.7 = (f32[96256]{0:T(1024)S(1)}, f32[96256]{0:T(1024)}, u32[]{:S(2)}) copy-start(f32[96256]{0:T(1024)} %reshape.112) | copy-start | bytes 1155076
  1224.0 336.6 %copy-start.2 = (f32[140672]{0:T(1024)S(1)}, f32[140672]{0:T(1024)}, u32[]{:S(2)}) copy-start(f32[140672]{0:T(1024)} %param.15) | copy-start | bytes 1688068
  1224.0 336.6 %copy-start.12 = (f32[140672]{0:T(1024)S(1)}, f32[140672]{0:T(1024)}, u32[]{:S(2)}) copy-start(f32[140672]{0:T(1024)} %param.16) | copy-start | bytes 1688068
  1224.0 336.6 %copy-start.13 = (f32[140672]{0:T(1024)S(1)}, f32[140672]{0:T(1024)}, u32[]{:S(2)}) copy-start(f32[140672]{0:T(1024)} %param.17) | copy-start | bytes 1688068
Sparse Core Ops, SparseCore 0:
  23.9 33.9 reduce-scatter.14
  60.8 55.6 reduce-scatter.22
  362.1 33.4 all-gather.8
  397.9 35.2 all-gather.12
  435.4 90.6 reduce-scatter.16
  528.2 87.9 reduce-scatter.24
  634.0 27.7 reduce-scatter.26
  664.7 28.4 reduce-scatter.18
  708.9 22.3 reduce-scatter.30
  734.0 23.7 reduce-scatter.32
  760.0 47.0 all-gather.10
  809.2 45.9 all-gather.14
  858.1 33.9 reduce-scatter.20
  895.2 35.1 reduce-scatter.28
Sparse Core Ops, SparseCore 1:
  28.9 122.3 all-gather.16
  1224.1 293.1 all-reduce.3
where the time goes:
time: 1600 us; the launch traced here: 1570 us
  waiting for transfers between devices  761 us (48%)
  local copies, waits for them, and re-layouts  346 us (22%)
  other arithmetic  230 us (14%)
  blocking collectives  141 us (9%)
  matrix products  73.1 us (5%)
  between operations  19.4 us (1%)
    unnamed x19, waiting for transfers between devices  315 us
    concatenate x2, local copies, waits for them, and re-layouts, per_device(): jnp.concatenate([grad_w1.reshape(-1), grad_w2.reshape(-1), grad_w3.reshap...  272 us
    all_gather x1, other arithmetic, gather_weights(): lax.all_gather(params.astype(jnp.bfloat16), ('rows', 'cols'), axis=0, til...  191 us
    reduce_scatter x6, waiting for transfers between devices, aggregate(): lax.psum_scatter(jnp.dot(fwd_tile, gathered, preferred_element_type=jnp.f...  172 us
    all_gather x1, waiting for transfers between devices, gather_weights(): lax.all_gather(params.astype(jnp.bfloat16), ('rows', 'cols'), axis=0, til...  92.6 us
    all_gather x2, waiting for transfers between devices, aggregate_back(): row_grads = lax.all_gather(upstream, 'cols', axis=0, tiled=True)  80.1 us
    all_gather x2, waiting for transfers between devices, aggregate(): gathered = lax.all_gather(inputs, 'rows', axis=0, tiled=True)  61.1 us
    unnamed x48, local copies, waits for them, and re-layouts  42.4 us
  transfers between devices with their start and end apart: 16, of which 15 were waited for; matrix products, arithmetic and copies ran while one was open for 21% of the time, Pallas kernels for 0%

commit v1 on v0

v1 whole, which is shorter than its diff:
```python
import jax
import jax.numpy as jnp
from jax import lax
from jax.sharding import PartitionSpec as P

FIN = 100
HID = 2048
NCLS = 47
BLK = 128
MB = 2
STEP = 10
PARAMS = FIN * HID + HID * HID + HID * NCLS + 2 * HID + NCLS

LAMBDA = 1.0
CLIP_NORM = 0.01
BETA_ONE = 0.9
BETA_TWO = 0.95
EPSILON = 1e-08
WEIGHT_DECAY = 0.1
LEARN_RATE = 0.02

LANES = 128
UNIT = HID // LANES
BOTH = ("rows", "cols")
F32 = jnp.float32
BF16 = jnp.bfloat16


def swap(x, axis, bit):
    size = lax.axis_size(axis)
    return lax.ppermute(x, axis, [(i, i ^ bit) for i in range(size)])


def bits_of(size):
    return [1 << i for i in range(size.bit_length() - 1)]


def mm(left, right):
    return jnp.dot(left, right, preferred_element_type=F32)


def mm_t(left, right):
    return lax.dot_general(left, right, (((0,), (0,)), ((), ())), preferred_element_type=F32)


def mm_nt(left, right):
    return lax.dot_general(left, right, (((1,), (1,)), ((), ())), preferred_element_type=F32)


def take(x, axis, picks):
    return jnp.concatenate([lax.slice_in_dim(x, p, p + 1, axis=axis) for p in picks], axis)


def split_bit(x, axis, order, bit):
    keep = [j for j in order if not j & bit]
    at = {j: i for i, j in enumerate(order)}
    return (
        take(x, axis, [at[j] for j in keep]),
        take(x, axis, [at[j | bit] for j in keep]),
        keep,
    )


def gelu_back(pre_act, upstream):
    return jax.vjp(jax.nn.gelu, pre_act)[1](upstream)[0]


def total_over_all(row):
    count = lax.axis_size(BOTH)
    sent = jnp.broadcast_to(row[None, :, :], (count,) + row.shape)
    return jnp.sum(lax.all_to_all(sent, BOTH, split_axis=0, concat_axis=0, tiled=True), axis=0)


def per_device(features, adjacency, block_mask, diagonal, labels, train_mask, params, first_moment, second_moment):
    n_rows, n_cols = lax.axis_size("rows"), lax.axis_size("cols")
    n_z = n_cols // 2
    n_dev = n_rows * n_cols
    my_row, my_col = lax.axis_index("rows"), lax.axis_index("cols")
    me = my_row * n_cols + my_col
    ns = features.shape[1]
    z_bits, row_bits = bits_of(n_z), bits_of(n_rows)
    z_order = [0]
    for bit in reversed(z_bits):
        z_order = z_order + [j ^ bit for j in z_order]
    z_at = {j: i for i, j in enumerate(z_order)}

    n_own = params.shape[0] // LANES
    slot = -(-((n_own + UNIT - 2) // UNIT + 1) // 8) * 8
    shift = lax.rem(n_own * me, UNIT)
    own = lax.dynamic_update_slice(
        jnp.zeros((slot * UNIT, LANES), BF16), params.reshape(n_own, LANES).astype(BF16), (shift, 0)
    ).reshape(1, 1, slot, HID)
    for bit in reversed(z_bits):
        own = jnp.concatenate([own, swap(own, "cols", 2 * bit)], 1)
    halves = []
    for half, order_of in ((0, row_bits), (1, row_bits[1:] + row_bits[:1])):
        part = own[..., half * (HID // 2) : (half + 1) * (HID // 2)]
        order = [0]
        for bit in order_of:
            part = jnp.concatenate([part, swap(part, "rows", bit)], 0)
            order = order + [j ^ bit for j in order]
        at = {j: i for i, j in enumerate(order)}
        halves.append(take(part, 0, [at[j] for j in range(n_rows)]))
    near = jnp.concatenate(halves, -1).reshape(n_rows * n_z * slot, HID)
    far = swap(near, "cols", 1)

    def units_of(core):
        owner = (my_row ^ jnp.arange(n_rows))[:, None] * n_cols + (
            my_col ^ (2 * jnp.array(z_order) + core)
        )[None, :]
        start = (n_own * owner) // UNIT
        return (start[:, :, None] + jnp.arange(slot)[None, None, :]).reshape(-1)

    units = jnp.concatenate([units_of(0), units_of(1)])
    expand = (jnp.arange(HID)[:, None] == (units - FIN)[None, :]).astype(BF16)
    per_small = -(-(FIN + NCLS + 3) // n_dev)
    n_small = per_small * n_dev
    small_unit = jnp.arange(n_small)
    small_unit = jnp.where(small_unit < FIN, small_unit, small_unit + HID)
    n_near = near.shape[0]
    pick = (small_unit[:, None] == units[None, :]).astype(BF16)
    small = (mm(pick[:, :n_near], near) + mm(pick[:, n_near:], far)).astype(BF16)
    w_first = small[:FIN]
    w_third = small[FIN : FIN + NCLS].reshape(HID, NCLS)
    b_first, b_second, b_third = (small[FIN + NCLS + i].astype(F32) for i in range(3))
    b_third = b_third[:NCLS]

    counted = train_mask.astype(F32)
    node_total = jnp.sum(total_over_all(jnp.broadcast_to(jnp.sum(counted), (1, LANES)))[0, :1])

    tile = adjacency.reshape(MB, n_cols, ns, n_rows, ns) * block_mask.reshape(
        MB, n_cols, 1, n_rows, 1
    ).astype(BF16)
    tile = jnp.concatenate(
        [
            lax.dynamic_slice_in_dim(tile, my_col ^ (2 * j + core), 1, 1)
            for core in (0, 1)
            for j in z_order
        ],
        1,
    )
    tile = jnp.concatenate(
        [lax.dynamic_slice_in_dim(tile, my_row ^ j, 1, 3) for j in range(n_rows)], 3
    )
    tile = lax.optimization_barrier(tile.reshape(MB, n_cols * ns, n_rows * ns))
    by_z = tile.reshape(MB, 2, n_z, ns, n_rows * ns)
    strip = [by_z[:, :, 0]]
    for j in z_order[1:]:
        strip.append(swap(by_z[:, :, z_at[j]], "cols", 2 * j))
    strip = jnp.concatenate(strip, -1).reshape(MB, 2 * ns, n_z * n_rows * ns)

    def over_z(x):
        return jnp.stack([x] + [swap(x, "cols", 2 * j) for j in z_order[1:]])

    def over_rows(x):
        return [x] + [swap(x, "rows", j) for j in range(1, n_rows)]

    feats = jnp.concatenate(over_rows(features), 1)
    partial = jnp.einsum("mik,mkf->mif", tile, feats, preferred_element_type=F32)
    partial = partial.reshape(MB, 2, n_z, ns, FIN)
    partial = partial[:, 0] + swap(partial[:, 1], "cols", 1)
    g_one = partial[:, 0] + LAMBDA * diagonal[:, :, None] * features.astype(F32)
    for i, j in enumerate(z_order[1:], 1):
        g_one = g_one + swap(partial[:, i], "cols", 2 * j)
    g_one = g_one.astype(BF16)
    all_one = jnp.stack(over_rows(over_z(g_one)))
    all_one = all_one.transpose(2, 1, 0, 3, 4).reshape(MB * n_z * n_rows * ns, FIN)
    h_one = jax.nn.gelu(mm(all_one, w_first) + b_first).astype(BF16)
    h_one = h_one.reshape(MB, n_z * n_rows * ns, HID)
    g_one = g_one.reshape(MB * ns, FIN)
    z_one = mm(g_one, w_first) + b_first

    diag = diagonal.reshape(MB * ns, 1)
    partial = jnp.einsum("mik,mkf->mif", strip, h_one, preferred_element_type=F32)
    g_two = (
        partial[:, :ns]
        + swap(partial[:, ns:].astype(BF16), "cols", 1).astype(F32)
        + LAMBDA * diagonal[:, :, None] * h_one[:, :ns].astype(F32)
    )
    g_two = g_two.reshape(MB * ns, HID).astype(BF16)
    g_spread = mm(g_two, expand).astype(BF16)
    z_two = mm(g_spread[:, :n_near], near) + mm(g_spread[:, n_near:], far) + b_second
    h_two = jax.nn.gelu(z_two).astype(BF16)

    def side_by_side(x):
        return jnp.concatenate([x[:ns], x[ns:]], 1)

    q = mm(h_two, w_third).astype(BF16)
    all_q = jnp.stack(over_rows(over_z(side_by_side(q))))
    all_q = all_q.transpose(1, 0, 2, 3).reshape(n_z * n_rows * ns, MB, NCLS)
    partial = jnp.stack([mm(strip[m], all_q[:, m]) for m in range(MB)], 1)
    partial = partial.reshape(2 * ns, MB * NCLS)
    logits = partial[:ns] + swap(partial[ns:], "cols", 1)
    logits = jnp.concatenate([logits[:, :NCLS], logits[:, NCLS:]], 0)
    logits = logits + LAMBDA * diag * q.astype(F32) + b_third
    log_total = jax.nn.logsumexp(logits, axis=1)
    hits = labels.reshape(-1, 1) == jnp.arange(NCLS, dtype=jnp.int32)[None, :]
    picked = jnp.sum(jnp.where(hits, logits, 0.0), axis=1)
    counted = counted.reshape(-1)
    loss = jnp.sum(counted * (log_total - picked))
    d_logits = counted[:, None] * (jnp.exp(logits - log_total[:, None]) - hits.astype(F32)) / node_total
    d_bias_three = jnp.sum(d_logits, axis=0)
    d_s = d_logits.astype(BF16)

    pair = side_by_side(d_s)
    all_s = jnp.concatenate([over_z(pair), over_z(swap(pair, "cols", 1))], 0)
    all_s = all_s.reshape(n_cols * ns, MB, NCLS)
    partial = jnp.stack([mm_t(tile[m], all_s[:, m]) for m in range(MB)], 1)
    partial = partial.reshape(n_rows, ns, MB * NCLS)
    d_q = partial[0]
    for j in range(1, n_rows):
        d_q = d_q + swap(partial[j], "rows", j)
    d_q = jnp.concatenate([d_q[:, :NCLS], d_q[:, NCLS:]], 0)
    d_q = (d_q + LAMBDA * diag * d_s.astype(F32)).astype(BF16)
    d_w_three = mm_t(h_two, d_q)
    d_z = gelu_back(z_two, mm_nt(d_q, w_third))
    d_bias_two = jnp.sum(d_z, axis=0)
    d_zb = d_z.astype(BF16)

    d_g = jnp.concatenate([mm_nt(d_zb, near), mm_nt(d_zb, far)], 1).astype(BF16)
    d_g = mm_nt(d_g, expand).astype(BF16)

    d_w_one, d_bias_one = [], []
    n_cut = 2
    wide = HID // n_cut
    for cut in range(n_cut):
        d_w_cut = 0.0
        d_bias_cut = 0.0
        for m in range(MB):
            up = d_g[m * ns : (m + 1) * ns, cut * wide : (cut + 1) * wide]
            got = up[None]
            for bit in reversed(z_bits):
                got = jnp.concatenate([got, swap(got, "cols", 2 * bit)], 0)
            got = jnp.concatenate([got, swap(got, "cols", 1)], 0).reshape(n_cols * ns, wide)
            partial = mm_t(tile[m], got).reshape(n_rows, ns, wide)
            low = partial.astype(BF16)
            d_h = partial[0] + LAMBDA * diagonal[m][:, None] * up.astype(F32)
            for j in range(1, n_rows):
                d_h = d_h + swap(low[j], "rows", j).astype(F32)
            d_one = gelu_back(z_one[m * ns : (m + 1) * ns, cut * wide : (cut + 1) * wide], d_h)
            d_bias_cut = d_bias_cut + jnp.sum(d_one, axis=0)
            d_w_cut = d_w_cut + mm_t(g_one[m * ns : (m + 1) * ns], d_one.astype(BF16))
        d_w_one.append(d_w_cut)
        d_bias_one.append(d_bias_cut)
    d_w_one = jnp.concatenate(d_w_one, 1)
    d_bias_one = jnp.concatenate(d_bias_one)

    d_w = mm_t(g_spread, d_zb).reshape(2, n_rows, n_z, slot, HID)
    d_w = d_w[0] + swap(d_w[1].astype(BF16), "cols", 1).astype(F32)
    halves = []
    for half, order_of in ((0, row_bits), (1, row_bits[1:] + row_bits[:1])):
        part = d_w[..., half * (HID // 2) : (half + 1) * (HID // 2)]
        order = list(range(n_rows))
        for bit in order_of:
            kept, sent, order = split_bit(part, 0, order, bit)
            part = kept + swap(sent.astype(BF16), "rows", bit).astype(F32)
        halves.append(part[0])
    part = jnp.concatenate(halves, -1)
    order = z_order
    for bit in z_bits:
        kept, sent, order = split_bit(part, 0, order, bit)
        part = kept + swap(sent.astype(BF16), "cols", 2 * bit).astype(F32)
    own_grad = part[0]

    pad_bias = jnp.pad(d_bias_three, (0, HID - NCLS))
    d_small = jnp.concatenate(
        [
            d_w_one,
            d_w_three.reshape(NCLS, HID),
            d_bias_one[None],
            d_bias_two[None],
            pad_bias[None],
            jnp.zeros((n_small - FIN - NCLS - 3, HID), F32),
        ],
        0,
    ).astype(BF16)
    d_small = d_small.reshape(n_dev, per_small * UNIT, LANES)
    got = lax.all_to_all(d_small, BOTH, split_axis=0, concat_axis=0, tiled=True)
    got = jnp.sum(got.astype(F32), axis=0)
    low = got.astype(BF16)
    sent = jnp.broadcast_to(low[None], d_small.shape)
    d_small = lax.all_to_all(sent, BOTH, split_axis=0, concat_axis=0, tiled=True)
    d_small = d_small.reshape(n_small, HID)

    own_flat = lax.dynamic_slice(own_grad.reshape(slot * UNIT, LANES), (shift, 0), (n_own, LANES))
    squares = jnp.sum(own_flat * own_flat) + jnp.sum(low.astype(F32) ** 2)
    row = jnp.concatenate([squares[None], loss[None], d_bias_three, jnp.zeros((LANES - NCLS - 2,), F32)])
    row = total_over_all(row[None])[0]
    squares, loss_sum, class_sum = row[0], row[1], row[2 : 2 + NCLS]

    mine = (n_own * me) // UNIT + jnp.arange(slot)
    place = (mine[:, None] == small_unit[None, :]).astype(BF16)
    small_flat = lax.dynamic_slice(
        mm(place, d_small).reshape(slot * UNIT, LANES), (shift, 0), (n_own, LANES)
    )
    reduced = (own_flat + small_flat).reshape(-1)

    grad_norm = jnp.sqrt(squares)
    clip_scale = jnp.minimum(1.0, CLIP_NORM / (grad_norm + 1e-06))
    clipped = reduced * clip_scale
    class_bias_grad = class_sum * clip_scale
    new_first = BETA_ONE * first_moment + (1.0 - BETA_ONE) * clipped
    new_second = BETA_TWO * second_moment + (1.0 - BETA_TWO) * clipped * clipped
    correct_one = 1.0 - BETA_ONE**STEP
    correct_two = 1.0 - BETA_TWO**STEP
    step_size = new_first / correct_one / (jnp.sqrt(new_second / correct_two) + EPSILON)
    new_params = params - LEARN_RATE * (step_size + WEIGHT_DECAY * params)
    return (new_params, new_first, new_second, grad_norm, loss_sum, node_total, class_bias_grad)


def solution(mesh):
    in_specs = (
        P(None, ("rows", "cols"), None),
        P(None, "rows", None, "cols", None),
        P(None, "rows", None, "cols", None),
        P(None, ("rows", "cols")),
        P(None, ("rows", "cols")),
        P(None, ("rows", "cols")),
        P(("rows", "cols")),
        P(("rows", "cols")),
        P(("rows", "cols")),
    )
    out_specs = (P(("rows", "cols")), P(("rows", "cols")), P(("rows", "cols")), P(), P(), P(), P())
    return jax.shard_map(
        per_device, mesh=mesh, in_specs=in_specs, out_specs=out_specs, check_vma=False
    )
```

time: 1600 us -> 559 us (0.35); the launches traced: 1570 us -> 550 us
  waiting for transfers between devices: 761 us -> 243 us
  local copies, waits for them, and re-layouts: 346 us -> 54.8 us
  other arithmetic: 230 us -> 61.5 us
  blocking collectives: 141 us -> 0 us
  starting transfers between devices: 1.77 us -> 108 us
    unnamed x19 -> x0, waiting for transfers between devices: 315 us -> none
    concatenate x2 -> x7, local copies, waits for them, and re-layouts: 272 us -> 3.83 us  [the longest x1 2.23 us: per_device(): jnp.concatenate([d_w_one, d_w_three.reshape(NCLS, HID), d_bias_one[None],...]
    all_gather x5 -> x0, waiting for transfers between devices: 234 us -> none  [the longest x1 92.6 us: gather_weights(): lax.all_gather(params.astype(jnp.bfloat16), ('rows', 'cols'), axis=0, til...]
    reduce_scatter x8 -> x0, waiting for transfers between devices: 213 us -> none  [the longest x6 172 us: aggregate(): lax.psum_scatter(jnp.dot(fwd_tile, gathered, preferred_element_type=jnp.f...]
    ppermute x0 -> x72, waiting for transfers between devices: none -> 202 us  [swap(): return lax.ppermute(x, axis, [(i, i ^ bit) for i in range(size)])]
    all_gather x1 -> x0, other arithmetic: 191 us -> none  [gather_weights(): lax.all_gather(params.astype(jnp.bfloat16), ('rows', 'cols'), axis=0, til...]
    ppermute x0 -> x72, starting transfers between devices: none -> 94.8 us  [swap(): return lax.ppermute(x, axis, [(i, i ^ bit) for i in range(size)])]
    psum x2 -> x0, blocking collectives: 81.5 us -> none  [the longest x1 41.3 us: per_device(): lax.psum(jnp.sum(train_mask.astype(jnp.float32)), ('rows', 'cols'))]
  transfers between devices with their start and end apart: 16 -> 76, of which waited for: 15 -> 40; matrix products, arithmetic and copies ran while one was open for 21% -> 21% of each run, Pallas kernels for 0% -> 0%
where the time goes in v1:
time: 559 us; the launch traced here: 550 us
  waiting for transfers between devices  243 us (43%)
  starting transfers between devices  108 us (19%)
  matrix products  77.4 us (14%)
  other arithmetic  61.5 us (11%)
  local copies, waits for them, and re-layouts  54.8 us (10%)
  between operations  5.94 us (1%)
    ppermute x72, waiting for transfers between devices, swap(): return lax.ppermute(x, axis, [(i, i ^ bit) for i in range(size)])  202 us
    ppermute x72, starting transfers between devices, swap(): return lax.ppermute(x, axis, [(i, i ^ bit) for i in range(size)])  94.8 us
    dot_general x11, matrix products, mm(): return jnp.dot(left, right, preferred_element_type=F32)  40.5 us
    all_to_all x1, waiting for transfers between devices, per_device(): lax.all_to_all(sent, BOTH, split_axis=0, concat_axis=0, tiled=True)  19.1 us
    dot_general x4, matrix products, mm_nt(): lax.dot_general(left, right, (((1,), (1,)), ((), ())), preferred_element_...  15.6 us
    all_to_all x2, waiting for transfers between devices, total_over_all(): lax.all_to_all(sent, BOTH, split_axis=0, concat_axis=0, tiled=True)  13.3 us
    another operation x5, other arithmetic  13 us
  transfers between devices with their start and end apart: 76, of which 40 were waited for; matrix products, arithmetic and copies ran while one was open for 21% of the time, Pallas kernels for 0%

profile of v1, /device:TPU:0, one launch (start us, length us, event | category | flops | bytes accessed | tf_op | source)
XLA Modules:
  0.0 550.3 jit_solution(11977568154874849337)
XLA Ops:
  2.8 4.1 collective-permute-start.16
  6.9 13.3 %collective-permute-done.16 = bf16[1,1,72,2048]{3,2,1,0:T(8,128)(2,1)S(1)} collective-permute-done((bf16[1,1,72,2048]{3,2,1,0:T(8,128)(2,1)S(1)}, bf16[1,1,72,2048]{3,2,1,0:T(8,128)(2,1)S(1)}, u32[]{:S(2)}, u32[]{:S(2)}) %collective-permute-start.16) | collective-permute-done | bytes 294944 | tf_op jit(solution)/shard_map/ppermute | solution.py:31
  21.1 13.7 %collective-permute-done.17 = bf16[1,2,72,2048]{3,2,1,0:T(8,128)(2,1)S(1)} collective-permute-done((bf16[1,2,72,2048]{3,2,1,0:T(8,128)(2,1)S(1)}, bf16[1,2,72,2048]{3,2,1,0:T(8,128)(2,1)S(1)}, u32[]{:S(2)}, u32[]{:S(2)}) %collective-permute-start.17) | collective-permute-done | bytes 589856 | tf_op jit(solution)/shard_map/ppermute | solution.py:31
  41.5 8.3 %collective-permute-done.20 = bf16[1,4,72,1024]{3,2,1,0:T(8,128)(2,1)S(1)} collective-permute-done((bf16[1,4,72,1024]{3,2,1,0:T(8,128)(2,1)S(1)}, bf16[1,4,72,1024]{3,2,1,0:T(8,128)(2,1)S(1)}, u32[]{:S(2)}, u32[]{:S(2)}) %collective-permute-start.20) | collective-permute-done | bytes 589856 | tf_op jit(solution)/shard_map/ppermute | solution.py:31
  55.0 22.2 %collective-permute-done.21 = bf16[2,4,72,1024]{3,2,1,0:T(8,128)(2,1)S(1)} collective-permute-done((bf16[2,4,72,1024]{3,2,1,0:T(8,128)(2,1)S(1)}, bf16[2,4,72,1024]{3,2,1,0:T(8,128)(2,1)S(1)}, u32[]{:S(2)}, u32[]{:S(2)}) %collective-permute-start.21) | collective-permute-done | bytes 1179680 | tf_op jit(solution)/shard_map/ppermute | solution.py:31
  77.4 2.6 maximum_maximum_fusion
  80.2 5.3 constant_dynamic-slice_fusion.3
  85.6 5.9 %pad_maximum_fusion = bf16[2,8,128,4,128]{4,3,2,1,0:T(4,128)(2,1)} fusion(bf16[2,8,128,1,128]{4,3,2,1,0:T(2,128)(2,1)S(1)} %get-tuple-element.40, bf16[2,8,128,1,128]{4,3,2,1,0:T(2,128)(2,1)S(1)} %get-tuple-element.41, bf16[2,8,128,1,128]{4,3,2,1,0:T(2,128)(2,1)S(1)} %get-tuple-element.42, bf16[2,8,128,1,128]{4,3,2,1,0:T(2,128)(2,1)S(1)} %get-tuple-element.39), kind=kLoop, calls=%fused_computation.43 | loop fusion | flops 8388608 | bytes 4194304 | tf_op jit(solution)/shard_map/concatenate | solution.py:142
  91.5 3.0 reshape.345
  95.9 4.4 collective-permute-start
  110.7 2.9 collective-permute-start.9
  113.5 17.9 %collective-permute-done.7 = f32[2,128,100]{1,2,0:T(8,128)S(1)} collective-permute-done((f32[2,128,100]{1,2,0:T(8,128)S(1)}, f32[2,128,100]{1,2,0:T(8,128)S(1)}, u32[]{:S(2)}, u32[]{:S(2)}) %collective-permute-start.7) | collective-permute-done | bytes 102432 | tf_op jit(solution)/shard_map/ppermute | solution.py:31
  131.5 4.8 collective-permute-start.10
  146.9 3.5 collective-permute-done.13
  150.5 3.4 collective-permute-done.14
  158.1 3.5 fusion.46
  161.7 3.5 fusion.15
  165.3 14.7 %fusion.7 = bf16[4096,2048]{1,0:T(8,128)(2,1)} fusion(f32[2048]{0:T(1024)S(1)} %bitcast.298, bf16[4096,100]{0,1:T(8,128)(2,1)S(1)} %copy-done.35, bf16[160,2048]{1,0:T(8,128)(2,1)S(1)} %fusion.15), kind=kOutput, calls=%fused_computation.8 | convolution fusion | flops 1761607680 | bytes 18063360 | tf_op jit(solution)/shard_map/dot_general | solution.py:39
  180.0 8.7 %fusion.24 = f32[2,256,2048]{2,1,0:T(8,128)S(1)} fusion(bf16[2,2048,2048]{2,1,0:T(8,128)(2,1)} %bitcast.293, bf16[2,256,512]{2,1,0:T(8,128)(2,1)} %bitcast.9, bf16[2,256,512]{2,1,0:T(8,128)(2,1)} %bitcast.7, bf16[2,256,512]{2,1,0:T(8,128)(2,1)} %bitcast.5, bf16[2,256,512]{2,1,0:T(8,128)(2,1)S(1)} %bitcast.278), kind=kOutput, calls=%fused_computation.44 | convolution fusion | flops 4303355904 | bytes 23068672 | tf_op jit(solution)/shard_map/mik,mkf->mif/dot_general | solution.py:174
  193.7 2.9 all-to-all-start
  196.7 6.6 %all-to-all-done = f32[32,1,128]{2,1,0:T(1,128)S(1)} async-done(((f32[32,1,128]{2,1,0:T(1,128)}), f32[32,1,128]{2,1,0:T(1,128)S(1)}, u32[]{:S(2)}, u32[]{:S(2)}) %all-to-all-start) | async-done | bytes 16416 | tf_op jit(solution)/shard_map/all_to_all | solution.py:71
  204.8 2.9 fusion.23
  207.8 3.9 fusion.12
  211.7 4.3 fusion.49
  216.0 5.9 %multiply_convert_fusion = (bf16[256,2048]{1,0:T(8,128)(2,1)S(1)}, f32[256,2048]{1,0:T(8,128)}) fusion(f32[2048]{0:T(1024)S(1)} %bitcast.306, f32[256,2048]{1,0:T(8,128)S(1)} %fusion.49, bf16[1152,2048]{1,0:T(8,128)(2,1)} %bitcast.22, bf16[256,2304]{1,0:T(8,128)(2,1)S(1)} %fusion.12), kind=kOutput, calls=%fused_computation.57 | convolution fusion | flops 1213726720 | bytes 10559488 | tf_op jit(solution)/shard_map/dot_general | solution.py:39
  223.6 3.2 collective-permute-start.26
  230.5 2.4 collective-permute-start.29
  244.3 3.1 collective-permute-start.32
  248.9 2.8 collective-permute-start.36
  253.6 3.8 collective-permute-done.37
  264.0 2.3 collective-permute-done.40
  266.4 3.9 fusion.177
  270.3 3.9 convolution_convert_fusion.1
  274.2 3.9 convolution_convert_fusion
  278.1 3.9 fusion.14
  283.0 2.8 collective-permute-start.48
  286.0 17.2 %collective-permute-done.60 = bf16[1,128,1024]{2,1,0:T(8,128)(2,1)S(1)} collective-permute-done((bf16[1,128,1024]{2,1,0:T(8,128)(2,1)S(1)}, bf16[1,128,1024]{2,1,0:T(8,128)(2,1)S(1)}, u32[]{:S(2)}, u32[]{:S(2)}) %collective-permute-start.60) | collective-permute-done | bytes 262176 | tf_op jit(solution)/shard_map/ppermute | solution.py:31
  306.2 3.4 collective-permute-start.54
  310.5 4.0 collective-permute-done.66
  316.5 14.8 %collective-permute-done.61 = bf16[2,128,1024]{2,1,0:T(8,128)(2,1)S(1)} collective-permute-done((bf16[2,128,1024]{2,1,0:T(8,128)(2,1)S(1)}, bf16[2,128,1024]{2,1,0:T(8,128)(2,1)S(1)}, u32[]{:S(2)}, u32[]{:S(2)}) %collective-permute-start.61) | collective-permute-done | bytes 524320 | tf_op jit(solution)/shard_map/ppermute | solution.py:31
  332.4 2.8 fusion.140
  335.2 2.8 slice.692
  338.1 4.4 slice.514
  349.1 4.7 collective-permute-done.67
  355.1 9.8 %collective-permute-done.55 = bf16[2,128,1024]{2,1,0:T(8,128)(2,1)S(1)} collective-permute-done((bf16[2,128,1024]{2,1,0:T(8,128)(2,1)S(1)}, bf16[2,128,1024]{2,1,0:T(8,128)(2,1)S(1)}, u32[]{:S(2)}, u32[]{:S(2)}) %collective-permute-start.55) | collective-permute-done | bytes 524320 | tf_op jit(solution)/shard_map/ppermute | solution.py:31
  371.4 2.8 collective-permute-start.65
  380.2 5.5 collective-permute-start.53
  386.2 3.6 collective-permute-done.51
  391.8 5.2 collective-permute-start.71
  397.5 3.6 collective-permute-done.69
  401.7 6.4 %collective-permute-start.59 = (bf16[128,1024]{1,0:T(8,128)(2,1)S(1)}, bf16[128,1024]{1,0:T(8,128)(2,1)S(1)}, u32[]{:S(2)}, u32[]{:S(2)}) collective-permute-start(bf16[128,1024]{1,0:T(8,128)(2,1)S(1)} %get-tuple-element.55), channel_id=1, source_target_pairs={{0,24},{8,16},{16,8},{24,0},{1,25},{9,17},{17,9},{25,1},{2,26},{10... | collective-permute-start | bytes 786440 | tf_op jit(solution)/shard_map/ppermute | solution.py:31
  409.3 3.1 collective-permute-done.57
  412.4 4.9 collective-permute-done.59
  419.4 12.9 %fusion.155 = (bf16[4,4,72,2048]{3,2,1,0:T(8,128)(2,1)}, f32[4,4,72,2048]{3,2,1,0:T(8,128)}) fusion(f32[4,4,72,2048]{3,2,1,0:T(8,128)} %bitcast.267, bf16[4,4,72,2048]{3,2,1,0:T(8,128)(2,1)} %collective-permute-done.41), kind=kLoop, calls=%fused_computation.329 | loop fusion | flops 7077888 | bytes 28311552 | tf_op jit(solution)/shard_map/convert.31
  439.5 21.4 %collective-permute-done.44 = bf16[2,4,72,1024]{3,2,1,0:T(8,128)(2,1)S(1)} collective-permute-done((bf16[2,4,72,1024]{3,2,1,0:T(8,128)(2,1)S(1)}, bf16[2,4,72,1024]{3,2,1,0:T(8,128)(2,1)S(1)}, u32[]{:S(2)}, u32[]{:S(2)}) %collective-permute-start.44) | collective-permute-done | bytes 1179680 | tf_op jit(solution)/shard_map/ppermute | solution.py:31
  472.8 3.3 all-to-all-start.1
  479.2 6.5 %collective-permute-done.43 = bf16[1,4,72,1024]{3,2,1,0:T(8,128)(2,1)} collective-permute-done((bf16[1,4,72,1024]{3,2,1,0:T(8,128)(2,1)}, bf16[1,4,72,1024]{3,2,1,0:T(8,128)(2,1)}, u32[]{:S(2)}, u32[]{:S(2)}) %collective-permute-start.43) | collective-permute-done | bytes 589856 | tf_op jit(solution)/shard_map/ppermute | solution.py:31
  487.1 8.2 %all-to-all-done.1 = bf16[32,80,128]{2,1,0:T(8,128)(2,1)} async-done(((bf16[32,80,128]{2,1,0:T(8,128)(2,1)}), bf16[32,80,128]{2,1,0:T(8,128)(2,1)}, u32[]{:S(2)}, u32[]{:S(2)}) %all-to-all-start.1) | async-done | bytes 655392 | tf_op jit(solution)/shard_map/all_to_all | solution.py:278
  497.4 3.3 all-to-all-start.2
  503.4 2.5 collective-permute-start.47
  507.1 19.1 %all-to-all-done.2 = bf16[32,80,128]{2,1,0:T(8,128)(2,1)} async-done(((bf16[32,80,128]{2,1,0:T(8,128)(2,1)}), bf16[32,80,128]{2,1,0:T(8,128)(2,1)}, u32[]{:S(2)}, u32[]{:S(2)}) %all-to-all-start.2) | async-done | bytes 655392 | tf_op jit(solution)/shard_map/all_to_all | solution.py:282
  527.6 3.5 collective-permute-done.47
  534.7 3.5 all-to-all-start.3
  538.6 6.7 %all-to-all-done.3 = f32[32,1,128]{2,1,0:T(1,128)S(1)} async-done(((f32[32,1,128]{2,1,0:T(1,128)}), f32[32,1,128]{2,1,0:T(1,128)S(1)}, u32[]{:S(2)}, u32[]{:S(2)}) %all-to-all-start.3) | async-done | bytes 16416 | tf_op jit(solution)/shard_map/all_to_all | solution.py:71
  (433 shorter events, 146.0 us)
Async XLA Ops:
  2.8 17.4 %collective-permute-start.16 = (bf16[1,1,72,2048]{3,2,1,0:T(8,128)(2,1)S(1)}, bf16[1,1,72,2048]{3,2,1,0:T(8,128)(2,1)S(1)}, u32[]{:S(2)}, u32[]{:S(2)}) collective-permute-start(bf16[1,1,72,2048]{3,2,1,0:T(8,128)(2,1)S(1)} %reshape.349), channel_id=1, source_target_pairs={{0,4},{1,5},{2,6},{3,7},{4,0},{5,1},{6,2},{7,3},{8,12},{9,13},{10,... | collective-permute-start | bytes 884744 | tf_op jit(solution)/shard_map/ppermute | solution.py:31
  20.3 14.6 %collective-permute-start.17 = (bf16[1,2,72,2048]{3,2,1,0:T(8,128)(2,1)S(1)}, bf16[1,2,72,2048]{3,2,1,0:T(8,128)(2,1)S(1)}, u32[]{:S(2)}, u32[]{:S(2)}) collective-permute-start(bf16[1,2,72,2048]{3,2,1,0:T(8,128)(2,1)S(1)} %pad_maximum_fusion.14), channel_id=1, source_target_pairs={{0,2},{1,3},{2,0},{3,1},{4,6},{5,7},{6,4},{7,5},{8,10},{9,11},{10,... | collective-permute-start | bytes 1769480 | tf_op jit(solution)/shard_map/ppermute | solution.py:31
  35.0 14.8 %collective-permute-start.20 = (bf16[1,4,72,1024]{3,2,1,0:T(8,128)(2,1)S(1)}, bf16[1,4,72,1024]{3,2,1,0:T(8,128)(2,1)S(1)}, u32[]{:S(2)}, u32[]{:S(2)}) collective-permute-start(bf16[1,4,72,1024]{3,2,1,0:T(8,128)(2,1)S(1)} %get-tuple-element.44), channel_id=1, source_target_pairs={{0,16},{8,24},{16,0},{24,8},{1,17},{9,25},{17,1},{25,9},{2,18},{10... | collective-permute-start | bytes 1769480 | tf_op jit(solution)/shard_map/ppermute | solution.py:31
  36.3 16.3 %collective-permute-start.18 = (bf16[1,4,72,1024]{3,2,1,0:T(8,128)(2,1)S(1)}, bf16[1,4,72,1024]{3,2,1,0:T(8,128)(2,1)S(1)}, u32[]{:S(2)}, u32[]{:S(2)}) collective-permute-start(bf16[1,4,72,1024]{3,2,1,0:T(8,128)(2,1)S(1)} %get-tuple-element.43), channel_id=1, source_target_pairs={{0,8},{8,0},{16,24},{24,16},{1,9},{9,1},{17,25},{25,17},{2,10},{10... | collective-permute-start | bytes 1769480 | tf_op jit(solution)/shard_map/ppermute | solution.py:31
  37.9 62.6 %collective-permute-start.3 = (bf16[2,128,100]{1,2,0:T(8,128)(2,1)S(1)}, bf16[2,128,100]{1,2,0:T(8,128)(2,1)S(1)}, u32[]{:S(2)}, u32[]{:S(2)}) collective-permute-start(bf16[2,128,100]{1,2,0:T(8,128)(2,1)S(1)} %copy.139), channel_id=1, source_target_pairs={{0,8},{8,0},{16,24},{24,16},{1,9},{9,1},{17,25},{25,17},{2,10},{10... | collective-permute-start | bytes 153608 | tf_op jit(solution)/shard_map/ppermute | solution.py:31
  38.4 62.1 %collective-permute-start.4 = (bf16[2,128,100]{1,2,0:T(8,128)(2,1)S(1)}, bf16[2,128,100]{1,2,0:T(8,128)(2,1)S(1)}, u32[]{:S(2)}, u32[]{:S(2)}) collective-permute-start(bf16[2,128,100]{1,2,0:T(8,128)(2,1)S(1)} %copy.139), channel_id=1, source_target_pairs={{0,16},{8,24},{16,0},{24,8},{1,17},{9,25},{17,1},{25,9},{2,18},{10... | collective-permute-start | bytes 153608 | tf_op jit(solution)/shard_map/ppermute | solution.py:31
  39.2 62.5 %collective-permute-start.5 = (bf16[2,128,100]{1,2,0:T(8,128)(2,1)S(1)}, bf16[2,128,100]{1,2,0:T(8,128)(2,1)}, u32[]{:S(2)}, u32[]{:S(2)}) collective-permute-start(bf16[2,128,100]{1,2,0:T(8,128)(2,1)S(1)} %copy.139), channel_id=1, source_target_pairs={{0,24},{8,16},{16,8},{24,0},{1,25},{9,17},{17,9},{25,1},{2,26},{10... | collective-permute-start | bytes 153608 | tf_op jit(solution)/shard_map/ppermute | solution.py:31
  49.9 27.3 %collective-permute-start.21 = (bf16[2,4,72,1024]{3,2,1,0:T(8,128)(2,1)S(1)}, bf16[2,4,72,1024]{3,2,1,0:T(8,128)(2,1)S(1)}, u32[]{:S(2)}, u32[]{:S(2)}) collective-permute-start(bf16[2,4,72,1024]{3,2,1,0:T(8,128)(2,1)S(1)} %pad_maximum_fusion.8), channel_id=1, source_target_pairs={{0,8},{8,0},{16,24},{24,16},{1,9},{9,1},{17,25},{25,17},{2,10},{10... | collective-permute-start | bytes 3538952 | tf_op jit(solution)/shard_map/ppermute | solution.py:31
  52.7 24.6 %collective-permute-start.19 = (bf16[2,4,72,1024]{3,2,1,0:T(8,128)(2,1)S(1)}, bf16[2,4,72,1024]{3,2,1,0:T(8,128)(2,1)S(1)}, u32[]{:S(2)}, u32[]{:S(2)}) collective-permute-start(bf16[2,4,72,1024]{3,2,1,0:T(8,128)(2,1)S(1)} %pad_maximum_fusion.7), channel_id=1, source_target_pairs={{0,16},{8,24},{16,0},{24,8},{1,17},{9,25},{17,1},{25,9},{2,18},{10... | collective-permute-start | bytes 3538952 | tf_op jit(solution)/shard_map/ppermute | solution.py:31
  80.0 78.1 %collective-permute-start.22 = (bf16[1152,2048]{1,0:T(8,128)(2,1)}, bf16[1152,2048]{1,0:T(8,128)(2,1)}, u32[]{:S(2)}, u32[]{:S(2)}) collective-permute-start(bf16[1152,2048]{1,0:T(8,128)(2,1)} %bitcast.22), channel_id=1, source_target_pairs={{0,1},{1,0},{2,3},{3,2},{4,5},{5,4},{6,7},{7,6},{8,9},{9,8},{10,11... | collective-permute-start | bytes 14155784 | tf_op jit(solution)/shard_map/ppermute | solution.py:31
  95.9 84.1 %collective-permute-start = (bf16[2,2,128,512]{3,2,1,0:T(8,128)(2,1)}, bf16[2,2,128,512]{3,2,1,0:T(8,128)(2,1)}, u32[]{:S(2)}, u32[]{:S(2)}) collective-permute-start(bf16[2,2,128,512]{3,2,1,0:T(8,128)(2,1)} %get-tuple-element.36), channel_id=1, source_target_pairs={{0,4},{1,5},{2,6},{3,7},{4,0},{5,1},{6,2},{7,3},{8,12},{9,13},{10,... | collective-permute-start | bytes 1572872 | tf_op jit(solution)/shard_map/ppermute | solution.py:31
  108.9 22.5 %collective-permute-start.7 = (f32[2,128,100]{1,2,0:T(8,128)S(1)}, f32[2,128,100]{1,2,0:T(8,128)S(1)}, u32[]{:S(2)}, u32[]{:S(2)}) collective-permute-start(f32[2,128,100]{1,2,0:T(8,128)S(1)} %bitcast.285), channel_id=1, source_target_pairs={{0,4},{1,5},{2,6},{3,7},{4,0},{5,1},{6,2},{7,3},{8,12},{9,13},{10,... | collective-permute-start | bytes 307208 | tf_op jit(solution)/shard_map/ppermute | solution.py:31
  109.2 22.3 %collective-permute-start.8 = (f32[2,128,100]{1,2,0:T(8,128)S(1)}, f32[2,128,100]{1,2,0:T(8,128)S(1)}, u32[]{:S(2)}, u32[]{:S(2)}) collective-permute-start(f32[2,128,100]{1,2,0:T(8,128)S(1)} %bitcast.286), channel_id=1, source_target_pairs={{0,2},{1,3},{2,0},{3,1},{4,6},{5,7},{6,4},{7,5},{8,10},{9,11},{10,... | collective-permute-start | bytes 307208 | tf_op jit(solution)/shard_map/ppermute | solution.py:31
  110.7 20.8 %collective-permute-start.9 = (f32[2,128,100]{1,2,0:T(8,128)S(1)}, f32[2,128,100]{1,2,0:T(8,128)S(1)}, u32[]{:S(2)}, u32[]{:S(2)}) collective-permute-start(f32[2,128,100]{1,2,0:T(8,128)S(1)} %bitcast.287), channel_id=1, source_target_pairs={{0,6},{1,7},{2,4},{3,5},{4,2},{5,3},{6,0},{7,1},{8,14},{9,15},{10,... | collective-permute-start | bytes 307208 | tf_op jit(solution)/shard_map/ppermute | solution.py:31
  131.5 8.0 %collective-permute-start.10 = (bf16[2,128,100]{1,2,0:T(8,128)(2,1)S(1)}, bf16[2,128,100]{1,2,0:T(8,128)(2,1)S(1)}, u32[]{:S(2)}, u32[]{:S(2)}) collective-permute-start(bf16[2,128,100]{1,2,0:T(8,128)(2,1)S(1)} %fusion.110), channel_id=1, source_target_pairs={{0,4},{1,5},{2,6},{3,7},{4,0},{5,1},{6,2},{7,3},{8,12},{9,13},{10,... | collective-permute-start | bytes 153608 | tf_op jit(solution)/shard_map/ppermute | solution.py:31
  136.3 6.0 %collective-permute-start.12 = (bf16[2,128,100]{1,2,0:T(8,128)(2,1)S(1)}, bf16[2,128,100]{1,2,0:T(8,128)(2,1)S(1)}, u32[]{:S(2)}, u32[]{:S(2)}) collective-permute-start(bf16[2,128,100]{1,2,0:T(8,128)(2,1)S(1)} %fusion.110), channel_id=1, source_target_pairs={{0,6},{1,7},{2,4},{3,5},{4,2},{5,3},{6,0},{7,1},{8,14},{9,15},{10,... | collective-permute-start | bytes 153608 | tf_op jit(solution)/shard_map/ppermute | solution.py:31
  142.4 8.1 %collective-permute-start.13 = (bf16[4,2,128,100]{2,3,1,0:T(8,128)(2,1)S(1)}, bf16[4,2,128,100]{2,3,1,0:T(8,128)(2,1)S(1)}, u32[]{:S(2)}, u32[]{:S(2)}) collective-permute-start(bf16[4,2,128,100]{2,3,1,0:T(8,128)(2,1)S(1)} %get-tuple-element.70), channel_id=1, source_target_pairs={{0,8},{8,0},{16,24},{24,16},{1,9},{9,1},{17,25},{25,17},{2,10},{10... | collective-permute-start | bytes 614408 | tf_op jit(solution)/shard_map/ppermute | solution.py:31
  143.9 9.9 %collective-permute-start.14 = (bf16[4,2,128,100]{2,3,1,0:T(8,128)(2,1)S(1)}, bf16[4,2,128,100]{2,3,1,0:T(8,128)(2,1)S(1)}, u32[]{:S(2)}, u32[]{:S(2)}) collective-permute-start(bf16[4,2,128,100]{2,3,1,0:T(8,128)(2,1)S(1)} %get-tuple-element.70), channel_id=1, source_target_pairs={{0,16},{8,24},{16,0},{24,8},{1,17},{9,25},{17,1},{25,9},{2,18},{10... | collective-permute-start | bytes 614408 | tf_op jit(solution)/shard_map/ppermute | solution.py:31
  144.4 11.5 %collective-permute-start.15 = (bf16[4,2,128,100]{2,3,1,0:T(8,128)(2,1)S(1)}, bf16[4,2,128,100]{2,3,1,0:T(8,128)(2,1)S(1)}, u32[]{:S(2)}, u32[]{:S(2)}) collective-permute-start(bf16[4,2,128,100]{2,3,1,0:T(8,128)(2,1)S(1)} %get-tuple-element.70), channel_id=1, source_target_pairs={{0,24},{8,16},{16,8},{24,0},{1,25},{9,17},{17,9},{25,1},{2,26},{10... | collective-permute-start | bytes 614408 | tf_op jit(solution)/shard_map/ppermute | solution.py:31
  150.5 29.6 %collective-permute-start.1 = (bf16[2,2,128,512]{3,2,1,0:T(8,128)(2,1)}, bf16[2,2,128,512]{3,2,1,0:T(8,128)(2,1)}, u32[]{:S(2)}, u32[]{:S(2)}) collective-permute-start(bf16[2,2,128,512]{3,2,1,0:T(8,128)(2,1)} %get-tuple-element.35), channel_id=1, source_target_pairs={{0,2},{1,3},{2,0},{3,1},{4,6},{5,7},{6,4},{7,5},{8,10},{9,11},{10,... | collective-permute-start | bytes 1572872 | tf_op jit(solution)/shard_map/ppermute | solution.py:31
  153.8 26.2 %collective-permute-start.2 = (bf16[2,2,128,512]{3,2,1,0:T(8,128)(2,1)}, bf16[2,2,128,512]{3,2,1,0:T(8,128)(2,1)}, u32[]{:S(2)}, u32[]{:S(2)}) collective-permute-start(bf16[2,2,128,512]{3,2,1,0:T(8,128)(2,1)} %get-tuple-element.38), channel_id=1, source_target_pairs={{0,6},{1,7},{2,4},{3,5},{4,2},{5,3},{6,0},{7,1},{8,14},{9,15},{10,... | collective-permute-start | bytes 1572872 | tf_op jit(solution)/shard_map/ppermute | solution.py:31
  191.8 13.0 %collective-permute-start.23 = (bf16[2,128,2048]{2,1,0:T(8,128)(2,1)}, bf16[2,128,2048]{2,1,0:T(8,128)(2,1)}, u32[]{:S(2)}, u32[]{:S(2)}) collective-permute-start(bf16[2,128,2048]{2,1,0:T(8,128)(2,1)} %slice.693), channel_id=1, source_target_pairs={{0,1},{1,0},{2,3},{3,2},{4,5},{5,4},{6,7},{7,6},{8,9},{9,8},{10,11... | collective-permute-start | bytes 3145736 | tf_op jit(solution)/shard_map/ppermute | solution.py:31
  193.7 9.6 %all-to-all-start = ((f32[32,1,128]{2,1,0:T(1,128)}), f32[32,1,128]{2,1,0:T(1,128)S(1)}, u32[]{:S(2)}, u32[]{:S(2)}) async-start(f32[32,1,128]{2,1,0:T(1,128)} %broadcast_in_dim_broadcast_in_dim_broadcast_in_dim.3), calls=%async_computation | async-start | bytes 32768 | tf_op jit(solution)/shard_map/all_to_all | solution.py:71
  222.4 6.1 %collective-permute-start.24 = (bf16[128,94]{0,1:T(8,128)(2,1)S(1)}, bf16[128,94]{0,1:T(8,128)(2,1)S(1)}, u32[]{:S(2)}, u32[]{:S(2)}) collective-permute-start(bf16[128,94]{0,1:T(8,128)(2,1)S(1)} %get-tuple-element.87), channel_id=1, source_target_pairs={{0,4},{1,5},{2,6},{3,7},{4,0},{5,1},{6,2},{7,3},{8,12},{9,13},{10,... | collective-permute-start | bytes 72200 | tf_op jit(solution)/shard_map/ppermute | solution.py:31
  223.6 5.6 %collective-permute-start.26 = (bf16[128,94]{0,1:T(8,128)(2,1)S(1)}, bf16[128,94]{0,1:T(8,128)(2,1)S(1)}, u32[]{:S(2)}, u32[]{:S(2)}) collective-permute-start(bf16[128,94]{0,1:T(8,128)(2,1)S(1)} %get-tuple-element.87), channel_id=1, source_target_pairs={{0,6},{1,7},{2,4},{3,5},{4,2},{5,3},{6,0},{7,1},{8,14},{9,15},{10,... | collective-permute-start | bytes 72200 | tf_op jit(solution)/shard_map/ppermute | solution.py:31
  230.5 5.5 %collective-permute-start.29 = (bf16[4,128,94]{1,2,0:T(8,128)(2,1)S(1)}, bf16[4,128,94]{1,2,0:T(8,128)(2,1)S(1)}, u32[]{:S(2)}, u32[]{:S(2)}) collective-permute-start(bf16[4,128,94]{1,2,0:T(8,128)(2,1)S(1)} %get-tuple-element.78), channel_id=1, source_target_pairs={{0,24},{8,16},{16,8},{24,0},{1,25},{9,17},{17,9},{25,1},{2,26},{10... | collective-permute-start | bytes 288776 | tf_op jit(solution)/shard_map/ppermute | solution.py:31
  243.3 8.4 %collective-permute-start.31 = (bf16[128,94]{0,1:T(8,128)(2,1)S(1)}, bf16[128,94]{0,1:T(8,128)(2,1)S(1)}, u32[]{:S(2)}, u32[]{:S(2)}) collective-permute-start(bf16[128,94]{0,1:T(8,128)(2,1)S(1)} %pad_maximum_fusion.25), channel_id=1, source_target_pairs={{0,4},{1,5},{2,6},{3,7},{4,0},{5,1},{6,2},{7,3},{8,12},{9,13},{10,... | collective-permute-start | bytes 72200 | tf_op jit(solution)/shard_map/ppermute | solution.py:31
  244.3 8.0 %collective-permute-start.32 = (bf16[128,94]{0,1:T(8,128)(2,1)S(1)}, bf16[128,94]{0,1:T(8,128)(2,1)S(1)}, u32[]{:S(2)}, u32[]{:S(2)}) collective-permute-start(bf16[128,94]{0,1:T(8,128)(2,1)S(1)} %pad_maximum_fusion.25), channel_id=1, source_target_pairs={{0,2},{1,3},{2,0},{3,1},{4,6},{5,7},{6,4},{7,5},{8,10},{9,11},{10,... | collective-permute-start | bytes 72200 | tf_op jit(solution)/shard_map/ppermute | solution.py:31
  247.3 5.7 %collective-permute-start.33 = (bf16[128,94]{0,1:T(8,128)(2,1)S(1)}, bf16[128,94]{0,1:T(8,128)(2,1)S(1)}, u32[]{:S(2)}, u32[]{:S(2)}) collective-permute-start(bf16[128,94]{0,1:T(8,128)(2,1)S(1)} %pad_maximum_fusion.25), channel_id=1, source_target_pairs={{0,6},{1,7},{2,4},{3,5},{4,2},{5,3},{6,0},{7,1},{8,14},{9,15},{10,... | collective-permute-start | bytes 72200 | tf_op jit(solution)/shard_map/ppermute | solution.py:31
  251.7 5.6 %collective-permute-start.37 = (bf16[128,94]{0,1:T(8,128)(2,1)S(1)}, bf16[128,94]{0,1:T(8,128)(2,1)S(1)}, u32[]{:S(2)}, u32[]{:S(2)}) collective-permute-start(bf16[128,94]{0,1:T(8,128)(2,1)S(1)} %collective-permute-done.34), channel_id=1, source_target_pairs={{0,6},{1,7},{2,4},{3,5},{4,2},{5,3},{6,0},{7,1},{8,14},{9,15},{10,... | collective-permute-start | bytes 72200 | tf_op jit(solution)/shard_map/ppermute | solution.py:31
  282.2 21.0 %collective-permute-start.60 = (bf16[1,128,1024]{2,1,0:T(8,128)(2,1)S(1)}, bf16[1,128,1024]{2,1,0:T(8,128)(2,1)S(1)}, u32[]{:S(2)}, u32[]{:S(2)}) collective-permute-start(bf16[1,128,1024]{2,1,0:T(8,128)(2,1)S(1)} %get-tuple-element.52), channel_id=1, source_target_pairs={{0,4},{1,5},{2,6},{3,7},{4,0},{5,1},{6,2},{7,3},{8,12},{9,13},{10,... | collective-permute-start | bytes 786440 | tf_op jit(solution)/shard_map/ppermute | solution.py:31
  283.0 26.5 %collective-permute-start.48 = (bf16[1,128,1024]{2,1,0:T(8,128)(2,1)S(1)}, bf16[1,128,1024]{2,1,0:T(8,128)(2,1)S(1)}, u32[]{:S(2)}, u32[]{:S(2)}) collective-permute-start(bf16[1,128,1024]{2,1,0:T(8,128)(2,1)S(1)} %get-tuple-element.50), channel_id=1, source_target_pairs={{0,4},{1,5},{2,6},{3,7},{4,0},{5,1},{6,2},{7,3},{8,12},{9,13},{10,... | collective-permute-start | bytes 786440 | tf_op jit(solution)/shard_map/ppermute | solution.py:31
  285.9 28.6 %collective-permute-start.66 = (bf16[1,128,1024]{2,1,0:T(8,128)(2,1)S(1)}, bf16[1,128,1024]{2,1,0:T(8,128)(2,1)S(1)}, u32[]{:S(2)}, u32[]{:S(2)}) collective-permute-start(bf16[1,128,1024]{2,1,0:T(8,128)(2,1)S(1)} %get-tuple-element.51), channel_id=1, source_target_pairs={{0,4},{1,5},{2,6},{3,7},{4,0},{5,1},{6,2},{7,3},{8,12},{9,13},{10,... | collective-permute-start | bytes 786440 | tf_op jit(solution)/shard_map/ppermute | solution.py:31
  303.2 28.0 %collective-permute-start.61 = (bf16[2,128,1024]{2,1,0:T(8,128)(2,1)S(1)}, bf16[2,128,1024]{2,1,0:T(8,128)(2,1)S(1)}, u32[]{:S(2)}, u32[]{:S(2)}) collective-permute-start(bf16[2,128,1024]{2,1,0:T(8,128)(2,1)S(1)} %pad_maximum_fusion.17), channel_id=1, source_target_pairs={{0,2},{1,3},{2,0},{3,1},{4,6},{5,7},{6,4},{7,5},{8,10},{9,11},{10,... | collective-permute-start | bytes 1572872 | tf_op jit(solution)/shard_map/ppermute | solution.py:31
  306.2 36.3 %collective-permute-start.54 = (bf16[1,128,1024]{2,1,0:T(8,128)(2,1)S(1)}, bf16[1,128,1024]{2,1,0:T(8,128)(2,1)}, u32[]{:S(2)}, u32[]{:S(2)}) collective-permute-start(bf16[1,128,1024]{2,1,0:T(8,128)(2,1)S(1)} %get-tuple-element.53), channel_id=1, source_target_pairs={{0,4},{1,5},{2,6},{3,7},{4,0},{5,1},{6,2},{7,3},{8,12},{9,13},{10,... | collective-permute-start | bytes 786440 | tf_op jit(solution)/shard_map/ppermute | solution.py:31
  310.4 37.4 %collective-permute-start.49 = (bf16[2,128,1024]{2,1,0:T(8,128)(2,1)}, bf16[2,128,1024]{2,1,0:T(8,128)(2,1)}, u32[]{:S(2)}, u32[]{:S(2)}) collective-permute-start(bf16[2,128,1024]{2,1,0:T(8,128)(2,1)} %pad_maximum_fusion.15), channel_id=1, source_target_pairs={{0,2},{1,3},{2,0},{3,1},{4,6},{5,7},{6,4},{7,5},{8,10},{9,11},{10,... | collective-permute-start | bytes 1572872 | tf_op jit(solution)/shard_map/ppermute | solution.py:31
  316.1 37.8 %collective-permute-start.67 = (bf16[2,128,1024]{2,1,0:T(8,128)(2,1)}, bf16[2,128,1024]{2,1,0:T(8,128)(2,1)}, u32[]{:S(2)}, u32[]{:S(2)}) collective-permute-start(bf16[2,128,1024]{2,1,0:T(8,128)(2,1)} %pad_maximum_fusion.18), channel_id=1, source_target_pairs={{0,2},{1,3},{2,0},{3,1},{4,6},{5,7},{6,4},{7,5},{8,10},{9,11},{10,... | collective-permute-start | bytes 1572872 | tf_op jit(solution)/shard_map/ppermute | solution.py:31
  332.4 33.8 %collective-permute-start.62 = (bf16[4,128,1024]{2,1,0:T(8,128)(2,1)}, bf16[4,128,1024]{2,1,0:T(8,128)(2,1)}, u32[]{:S(2)}, u32[]{:S(2)}) collective-permute-start(bf16[4,128,1024]{2,1,0:T(8,128)(2,1)} %pad_maximum_fusion.12), channel_id=1, source_target_pairs={{0,1},{1,0},{2,3},{3,2},{4,5},{5,4},{6,7},{7,6},{8,9},{9,8},{10,11... | collective-permute-start | bytes 3145736 | tf_op jit(solution)/shard_map/ppermute | solution.py:31
  343.6 21.3 %collective-permute-start.55 = (bf16[2,128,1024]{2,1,0:T(8,128)(2,1)S(1)}, bf16[2,128,1024]{2,1,0:T(8,128)(2,1)S(1)}, u32[]{:S(2)}, u32[]{:S(2)}) collective-permute-start(bf16[2,128,1024]{2,1,0:T(8,128)(2,1)S(1)} %pad_maximum_fusion.16), channel_id=1, source_target_pairs={{0,2},{1,3},{2,0},{3,1},{4,6},{5,7},{6,4},{7,5},{8,10},{9,11},{10,... | collective-permute-start | bytes 1572872 | tf_op jit(solution)/shard_map/ppermute | solution.py:31
  347.3 72.1 %collective-permute-start.41 = (bf16[4,4,72,2048]{3,2,1,0:T(8,128)(2,1)}, bf16[4,4,72,2048]{3,2,1,0:T(8,128)(2,1)}, u32[]{:S(2)}, u32[]{:S(2)}) collective-permute-start(bf16[4,4,72,2048]{3,2,1,0:T(8,128)(2,1)} %bitcast.272), channel_id=1, source_target_pairs={{0,1},{1,0},{2,3},{3,2},{4,5},{5,4},{6,7},{7,6},{8,9},{9,8},{10,11... | collective-permute-start | bytes 14155784 | tf_op jit(solution)/shard_map/ppermute | solution.py:31
  349.0 20.6 %collective-permute-start.50 = (bf16[4,128,1024]{2,1,0:T(8,128)(2,1)S(1)}, bf16[4,128,1024]{2,1,0:T(8,128)(2,1)S(1)}, u32[]{:S(2)}, u32[]{:S(2)}) collective-permute-start(bf16[4,128,1024]{2,1,0:T(8,128)(2,1)S(1)} %pad_maximum_fusion.10), channel_id=1, source_target_pairs={{0,1},{1,0},{2,3},{3,2},{4,5},{5,4},{6,7},{7,6},{8,9},{9,8},{10,11... | collective-permute-start | bytes 3145736 | tf_op jit(solution)/shard_map/ppermute | solution.py:31
  355.0 16.5 %collective-permute-start.68 = (bf16[4,128,1024]{2,1,0:T(8,128)(2,1)S(1)}, bf16[4,128,1024]{2,1,0:T(8,128)(2,1)S(1)}, u32[]{:S(2)}, u32[]{:S(2)}) collective-permute-start(bf16[4,128,1024]{2,1,0:T(8,128)(2,1)S(1)} %pad_maximum_fusion.13), channel_id=1, source_target_pairs={{0,1},{1,0},{2,3},{3,2},{4,5},{5,4},{6,7},{7,6},{8,9},{9,8},{10,11... | collective-permute-start | bytes 3145736 | tf_op jit(solution)/shard_map/ppermute | solution.py:31
  366.1 12.0 %collective-permute-start.56 = (bf16[4,128,1024]{2,1,0:T(8,128)(2,1)S(1)}, bf16[4,128,1024]{2,1,0:T(8,128)(2,1)S(1)}, u32[]{:S(2)}, u32[]{:S(2)}) collective-permute-start(bf16[4,128,1024]{2,1,0:T(8,128)(2,1)S(1)} %pad_maximum_fusion.11), channel_id=1, source_target_pairs={{0,1},{1,0},{2,3},{3,2},{4,5},{5,4},{6,7},{7,6},{8,9},{9,8},{10,11... | collective-permute-start | bytes 3145736 | tf_op jit(solution)/shard_map/ppermute | solution.py:31
  369.3 10.3 %collective-permute-start.63 = (bf16[128,1024]{1,0:T(8,128)(2,1)S(1)}, bf16[128,1024]{1,0:T(8,128)(2,1)S(1)}, u32[]{:S(2)}, u32[]{:S(2)}) collective-permute-start(bf16[128,1024]{1,0:T(8,128)(2,1)S(1)} %get-tuple-element.57), channel_id=1, source_target_pairs={{0,8},{8,0},{16,24},{24,16},{1,9},{9,1},{17,25},{25,17},{2,10},{10... | collective-permute-start | bytes 786440 | tf_op jit(solution)/shard_map/ppermute | solution.py:31
  369.6 10.6 %collective-permute-start.64 = (bf16[128,1024]{1,0:T(8,128)(2,1)S(1)}, bf16[128,1024]{1,0:T(8,128)(2,1)S(1)}, u32[]{:S(2)}, u32[]{:S(2)}) collective-permute-start(bf16[128,1024]{1,0:T(8,128)(2,1)S(1)} %get-tuple-element.59), channel_id=1, source_target_pairs={{0,16},{8,24},{16,0},{24,8},{1,17},{9,25},{17,1},{25,9},{2,18},{10... | collective-permute-start | bytes 786440 | tf_op jit(solution)/shard_map/ppermute | solution.py:31
  371.4 14.3 %collective-permute-start.65 = (bf16[128,1024]{1,0:T(8,128)(2,1)S(1)}, bf16[128,1024]{1,0:T(8,128)(2,1)S(1)}, u32[]{:S(2)}, u32[]{:S(2)}) collective-permute-start(bf16[128,1024]{1,0:T(8,128)(2,1)S(1)} %get-tuple-element.58), channel_id=1, source_target_pairs={{0,24},{8,16},{16,8},{24,0},{1,25},{9,17},{17,9},{25,1},{2,26},{10... | collective-permute-start | bytes 786440 | tf_op jit(solution)/shard_map/ppermute | solution.py:31
  378.1 11.7 %collective-permute-start.51 = (bf16[128,1024]{1,0:T(8,128)(2,1)S(1)}, bf16[128,1024]{1,0:T(8,128)(2,1)S(1)}, u32[]{:S(2)}, u32[]{:S(2)}) collective-permute-start(bf16[128,1024]{1,0:T(8,128)(2,1)S(1)} %get-tuple-element.47), channel_id=1, source_target_pairs={{0,8},{8,0},{16,24},{24,16},{1,9},{9,1},{17,25},{25,17},{2,10},{10... | collective-permute-start | bytes 786440 | tf_op jit(solution)/shard_map/ppermute | solution.py:31
  379.6 12.2 %collective-permute-start.52 = (bf16[128,1024]{1,0:T(8,128)(2,1)S(1)}, bf16[128,1024]{1,0:T(8,128)(2,1)S(1)}, u32[]{:S(2)}, u32[]{:S(2)}) collective-permute-start(bf16[128,1024]{1,0:T(8,128)(2,1)S(1)} %get-tuple-element.49), channel_id=1, source_target_pairs={{0,16},{8,24},{16,0},{24,8},{1,17},{9,25},{17,1},{25,9},{2,18},{10... | collective-permute-start | bytes 786440 | tf_op jit(solution)/shard_map/ppermute | solution.py:31
  380.2 16.7 %collective-permute-start.53 = (bf16[128,1024]{1,0:T(8,128)(2,1)S(1)}, bf16[128,1024]{1,0:T(8,128)(2,1)S(1)}, u32[]{:S(2)}, u32[]{:S(2)}) collective-permute-start(bf16[128,1024]{1,0:T(8,128)(2,1)S(1)} %get-tuple-element.48), channel_id=1, source_target_pairs={{0,24},{8,16},{16,8},{24,0},{1,25},{9,17},{17,9},{25,1},{2,26},{10... | collective-permute-start | bytes 786440 | tf_op jit(solution)/shard_map/ppermute | solution.py:31
  385.7 15.4 %collective-permute-start.69 = (bf16[128,1024]{1,0:T(8,128)(2,1)S(1)}, bf16[128,1024]{1,0:T(8,128)(2,1)S(1)}, u32[]{:S(2)}, u32[]{:S(2)}) collective-permute-start(bf16[128,1024]{1,0:T(8,128)(2,1)S(1)} %get-tuple-element.60), channel_id=1, source_target_pairs={{0,8},{8,0},{16,24},{24,16},{1,9},{9,1},{17,25},{25,17},{2,10},{10... | collective-permute-start | bytes 786440 | tf_op jit(solution)/shard_map/ppermute | solution.py:31
  389.8 11.9 %collective-permute-start.70 = (bf16[128,1024]{1,0:T(8,128)(2,1)S(1)}, bf16[128,1024]{1,0:T(8,128)(2,1)S(1)}, u32[]{:S(2)}, u32[]{:S(2)}) collective-permute-start(bf16[128,1024]{1,0:T(8,128)(2,1)S(1)} %get-tuple-element.62), channel_id=1, source_target_pairs={{0,16},{8,24},{16,0},{24,8},{1,17},{9,25},{17,1},{25,9},{2,18},{10... | collective-permute-start | bytes 786440 | tf_op jit(solution)/shard_map/ppermute | solution.py:31
  391.8 17.5 %collective-permute-start.71 = (bf16[128,1024]{1,0:T(8,128)(2,1)S(1)}, bf16[128,1024]{1,0:T(8,128)(2,1)S(1)}, u32[]{:S(2)}, u32[]{:S(2)}) collective-permute-start(bf16[128,1024]{1,0:T(8,128)(2,1)S(1)} %get-tuple-element.61), channel_id=1, source_target_pairs={{0,24},{8,16},{16,8},{24,0},{1,25},{9,17},{17,9},{25,1},{2,26},{10... | collective-permute-start | bytes 786440 | tf_op jit(solution)/shard_map/ppermute | solution.py:31
  397.0 15.4 %collective-permute-start.57 = (bf16[128,1024]{1,0:T(8,128)(2,1)S(1)}, bf16[128,1024]{1,0:T(8,128)(2,1)S(1)}, u32[]{:S(2)}, u32[]{:S(2)}) collective-permute-start(bf16[128,1024]{1,0:T(8,128)(2,1)S(1)} %get-tuple-element.54), channel_id=1, source_target_pairs={{0,8},{8,0},{16,24},{24,16},{1,9},{9,1},{17,25},{25,17},{2,10},{10... | collective-permute-start | bytes 786440 | tf_op jit(solution)/shard_map/ppermute | solution.py:31
  401.1 11.3 %collective-permute-start.58 = (bf16[128,1024]{1,0:T(8,128)(2,1)S(1)}, bf16[128,1024]{1,0:T(8,128)(2,1)S(1)}, u32[]{:S(2)}, u32[]{:S(2)}) collective-permute-start(bf16[128,1024]{1,0:T(8,128)(2,1)S(1)} %get-tuple-element.56), channel_id=1, source_target_pairs={{0,16},{8,24},{16,0},{24,8},{1,17},{9,25},{17,1},{25,9},{2,18},{10... | collective-permute-start | bytes 786440 | tf_op jit(solution)/shard_map/ppermute | solution.py:31
  401.7 15.6 %collective-permute-start.59 = (bf16[128,1024]{1,0:T(8,128)(2,1)S(1)}, bf16[128,1024]{1,0:T(8,128)(2,1)S(1)}, u32[]{:S(2)}, u32[]{:S(2)}) collective-permute-start(bf16[128,1024]{1,0:T(8,128)(2,1)S(1)} %get-tuple-element.55), channel_id=1, source_target_pairs={{0,24},{8,16},{16,8},{24,0},{1,25},{9,17},{17,9},{25,1},{2,26},{10... | collective-permute-start | bytes 786440 | tf_op jit(solution)/shard_map/ppermute | solution.py:31
  433.6 27.3 %collective-permute-start.44 = (bf16[2,4,72,1024]{3,2,1,0:T(8,128)(2,1)S(1)}, bf16[2,4,72,1024]{3,2,1,0:T(8,128)(2,1)S(1)}, u32[]{:S(2)}, u32[]{:S(2)}) collective-permute-start(bf16[2,4,72,1024]{3,2,1,0:T(8,128)(2,1)S(1)} %concatenate.200), channel_id=1, source_target_pairs={{0,16},{8,24},{16,0},{24,8},{1,17},{9,25},{17,1},{25,9},{2,18},{10... | collective-permute-start | bytes 3538952 | tf_op jit(solution)/shard_map/ppermute | solution.py:31
  436.6 28.6 %collective-permute-start.42 = (bf16[2,4,72,1024]{3,2,1,0:T(8,128)(2,1)S(1)}, bf16[2,4,72,1024]{3,2,1,0:T(8,128)(2,1)S(1)}, u32[]{:S(2)}, u32[]{:S(2)}) collective-permute-start(bf16[2,4,72,1024]{3,2,1,0:T(8,128)(2,1)S(1)} %pad_maximum_fusion.9), channel_id=1, source_target_pairs={{0,8},{8,0},{16,24},{24,16},{1,9},{9,1},{17,25},{25,17},{2,10},{10... | collective-permute-start | bytes 3538952 | tf_op jit(solution)/shard_map/ppermute | solution.py:31
  463.9 14.0 %collective-permute-start.45 = (bf16[1,4,72,1024]{3,2,1,0:T(8,128)(2,1)}, bf16[1,4,72,1024]{3,2,1,0:T(8,128)(2,1)}, u32[]{:S(2)}, u32[]{:S(2)}) collective-permute-start(bf16[1,4,72,1024]{3,2,1,0:T(8,128)(2,1)} %slice.694), channel_id=1, source_target_pairs={{0,8},{8,0},{16,24},{24,16},{1,9},{9,1},{17,25},{25,17},{2,10},{10... | collective-permute-start | bytes 1769480 | tf_op jit(solution)/shard_map/ppermute | solution.py:31
  468.0 17.6 %collective-permute-start.43 = (bf16[1,4,72,1024]{3,2,1,0:T(8,128)(2,1)}, bf16[1,4,72,1024]{3,2,1,0:T(8,128)(2,1)}, u32[]{:S(2)}, u32[]{:S(2)}) collective-permute-start(bf16[1,4,72,1024]{3,2,1,0:T(8,128)(2,1)} %slice.695), channel_id=1, source_target_pairs={{0,16},{8,24},{16,0},{24,8},{1,17},{9,25},{17,1},{25,9},{2,18},{10... | collective-permute-start | bytes 1769480 | tf_op jit(solution)/shard_map/ppermute | solution.py:31
  472.8 22.5 %all-to-all-start.1 = ((bf16[32,80,128]{2,1,0:T(8,128)(2,1)}), bf16[32,80,128]{2,1,0:T(8,128)(2,1)}, u32[]{:S(2)}, u32[]{:S(2)}) async-start(bf16[32,80,128]{2,1,0:T(8,128)(2,1)} %convert_element_type.259), calls=%async_computation.1 | async-start | bytes 1310720 | tf_op jit(solution)/shard_map/all_to_all | solution.py:278
  487.0 15.1 %collective-permute-start.46 = (bf16[2,72,2048]{2,1,0:T(8,128)(2,1)S(1)}, bf16[2,72,2048]{2,1,0:T(8,128)(2,1)}, u32[]{:S(2)}, u32[]{:S(2)}) collective-permute-start(bf16[2,72,2048]{2,1,0:T(8,128)(2,1)S(1)} %fusion.36), channel_id=1, source_target_pairs={{0,2},{1,3},{2,0},{3,1},{4,6},{5,7},{6,4},{7,5},{8,10},{9,11},{10,... | collective-permute-start | bytes 1769480 | tf_op jit(solution)/shard_map/ppermute | solution.py:31
  497.4 28.8 %all-to-all-start.2 = ((bf16[32,80,128]{2,1,0:T(8,128)(2,1)}), bf16[32,80,128]{2,1,0:T(8,128)(2,1)}, u32[]{:S(2)}, u32[]{:S(2)}) async-start(bf16[32,80,128]{2,1,0:T(8,128)(2,1)} %broadcast_in_dim.92), calls=%async_computation.2 | async-start | bytes 1310720 | tf_op jit(solution)/shard_map/all_to_all | solution.py:282
  503.4 27.7 %collective-permute-start.47 = (bf16[1,72,2048]{2,1,0:T(8,128)(2,1)S(1)}, bf16[1,72,2048]{2,1,0:T(8,128)(2,1)S(1)}, u32[]{:S(2)}, u32[]{:S(2)}) collective-permute-start(bf16[1,72,2048]{2,1,0:T(8,128)(2,1)S(1)} %slice.696), channel_id=1, source_target_pairs={{0,4},{1,5},{2,6},{3,7},{4,0},{5,1},{6,2},{7,3},{8,12},{9,13},{10,... | collective-permute-start | bytes 884744 | tf_op jit(solution)/shard_map/ppermute | solution.py:31
  534.7 10.6 %all-to-all-start.3 = ((f32[32,1,128]{2,1,0:T(1,128)}), f32[32,1,128]{2,1,0:T(1,128)S(1)}, u32[]{:S(2)}, u32[]{:S(2)}) async-start(f32[32,1,128]{2,1,0:T(1,128)} %broadcast_in_dim.98), calls=%async_computation.3 | async-start | bytes 32768 | tf_op jit(solution)/shard_map/all_to_all | solution.py:71
  (84 other events, 1128.7 us)
